TPU v7x, 256 devices: a whole 4x4x8 slice. The times are simulated.
256 devices in a mesh: ctx: 32 (over y, z_lo, core), exp: 8 (over z_hi, x).
Axes of the slice: x: 4, y: 4, z: 8 (z_hi: 2, z_lo: 4; z = z_hi * 4 + z_lo), core: 2. Of those that a mesh axis runs over, the one named last changes fastest.
Arguments:
- tokens: bfloat16 [16384, 2048], P(('ctx', 'exp')), may hold values from -6 to 6
- attn_gain: bfloat16 [2048], replicated, may hold values from 0.25 to 1.75
- q_weight: bfloat16 [2048, 4096], P('ctx', 'exp'), may hold values from -0.125 to 0.125
- k_weight: bfloat16 [2048, 512], P('ctx'), may hold values from -0.125 to 0.125
- v_weight: bfloat16 [2048, 512], P('ctx'), may hold values from -0.125 to 0.125
- q_gain: bfloat16 [128], replicated, may hold values from 0.6 to 6, as said below
- k_gain: bfloat16 [128], replicated, may hold values from 0.6 to 6, as said below
- out_weight: bfloat16 [4096, 2048], P('exp', 'ctx'), may hold values from -0.09375 to 0.09375
- moe_gain: bfloat16 [2048], replicated, may hold values from 0.25 to 1.75
- expert_ids: int32 [16384, 2], P(('ctx', 'exp')), may hold values from 0 to 7, all different within a row; in each aligned block of 64 rows (0 to 63, 64 to 127, ...) at most 32 rows name the same one
- route_code: int32 [16384, 2], P(('ctx', 'exp')), may hold values from 1 to 1023
- gate_weight: bfloat16 [8, 2048, 768], P('exp'), may hold values from -0.125 to 0.125
- up_weight: bfloat16 [8, 2048, 768], P('exp'), may hold values from -0.125 to 0.125
- expert_down_matrix: bfloat16 [8, 768, 2048], P('exp'), may hold values from -0.21875 to 0.21875
Outputs:
- layer_out: bfloat16 [16384, 2048], P(('ctx', 'exp'))
Inputs may be any that keep to these rules, and one draw needn't show every extreme that they name: `expert_ids`: among the 64 rows of one device no expert is named by more than 32 rows, and in every draw some expert is named by exactly 32 rows of some device. `q_gain`: positive gains. `k_gain`: positive gains.
All inputs are finite; a program needn't handle non-finite values.
Results may differ from a plain program's by a relative error of at most 0.02.
The roundings to bfloat16 on the way count: a program that leaves them out, or rounds other values in their place, can miss the bound.
Values may be sent and summed in bfloat16 or wider, within the bound.
No kernel may reach another device: no remote copies, remote signals or barrier semaphores. Data moves between devices by JAX's collectives and lax.ppermute only.
A program may use at most 192 MiB of HBM per device.

v0:
```python
import math

import jax
import jax.numpy as jnp
from jax import lax
from jax.sharding import PartitionSpec as P


def normed(values, gain):
    widened = values.astype(jnp.float32)
    second_expert = jnp.mean(widened * widened, axis=-1, keepdims=True)
    return widened * lax.rsqrt(second_expert + 1e-06) * gain.astype(jnp.float32)


def shards(
    tokens,
    attn_gain,
    q_weight,
    k_weight,
    v_weight,
    q_gain,
    k_gain,
    out_weight,
    moe_gain,
    expert_ids,
    route_code,
    gate_weight,
    up_weight,
    expert_down_matrix,
):
    exp_count = lax.axis_size("exp")
    ctx_place = lax.axis_index("ctx")
    exp_place = lax.axis_index("exp")
    tok_rows, width = tokens.shape
    head_dim = q_gain.shape[0]
    query_cols = q_weight.shape[1]
    local_heads = query_cols // head_dim
    group_size = local_heads * exp_count // (k_weight.shape[1] // head_dim)
    local_kv = max(1, local_heads // group_size)
    per_kv = local_heads // local_kv
    kv_first = exp_place * local_heads // group_size
    kv_cols = local_kv * head_dim
    block_rows = tok_rows * exp_count
    scale_factor = 1.0 / math.sqrt(head_dim)
    normal_rows = normed(tokens, attn_gain).astype(jnp.bfloat16)
    block_tokens = lax.all_gather(normal_rows, "exp", axis=0, tiled=True)
    pieces = (
        lax.all_gather(q_weight, "ctx", axis=0, tiled=True),
        lax.all_gather(k_weight, "ctx", axis=0, tiled=True),
        lax.all_gather(v_weight, "ctx", axis=0, tiled=True),
    )
    key_part = lax.dynamic_slice_in_dim(pieces[1], kv_first * head_dim, kv_cols, 1)
    value_part = lax.dynamic_slice_in_dim(pieces[2], kv_first * head_dim, kv_cols, 1)
    query_sums = jnp.dot(block_tokens, pieces[0], preferred_element_type=jnp.float32)
    key_sums = jnp.dot(block_tokens, key_part, preferred_element_type=jnp.float32)
    value_sums = jnp.dot(block_tokens, value_part, preferred_element_type=jnp.float32)
    normal_keys = normed(key_sums.reshape(-1, local_kv, head_dim), k_gain).reshape(-1, kv_cols)
    travelling = jnp.concatenate([normal_keys, value_sums], axis=1).astype(jnp.bfloat16)
    queries = normed(query_sums.reshape(block_rows, local_heads, head_dim), q_gain).astype(
        jnp.bfloat16
    )
    positions = ctx_place * block_rows + jnp.arange(block_rows, dtype=jnp.int32)
    grouped_query_rows = queries.reshape(block_rows, local_kv, per_kv, head_dim)
    last_query = jnp.max(positions)
    initial = (
        jnp.full((local_kv, per_kv, block_rows), -1e30, jnp.float32),
        jnp.zeros((local_kv, per_kv, block_rows), jnp.float32),
        jnp.zeros((local_kv, per_kv, block_rows, head_dim), jnp.float32),
    )
    pieces = lax.all_gather(travelling, "ctx", axis=0, tiled=True)
    length = pieces.shape[0]
    stride = math.gcd(length, 512)
    turns = length // stride

    def one_block(turn, inner):
        key_start = turn * stride

        def compute(current):
            rows_in = lax.dynamic_slice_in_dim(pieces, turn * stride, stride, 0)
            resident_key_block = rows_in[:, :kv_cols].reshape(stride, local_kv, head_dim)
            values_here = rows_in[:, kv_cols:].reshape(stride, local_kv, head_dim)
            scores = (
                jnp.einsum(
                    "azpw,czw->zpac",
                    grouped_query_rows,
                    resident_key_block,
                    preferred_element_type=jnp.float32,
                )
                * scale_factor
            )
            key_positions = key_start + jnp.arange(stride, dtype=jnp.int32)
            allowed = key_positions[None, :] <= positions[:, None]
            masked = jnp.where(allowed, scores, -1e30)
            running, denominator, accumulated = current
            new_running = jnp.maximum(running, jnp.max(masked, axis=-1))
            weights = jnp.where(allowed, jnp.exp(masked - new_running[..., None]), 0.0)
            decay = jnp.exp(running - new_running)
            denominator = denominator * decay + jnp.sum(weights, axis=-1)
            accumulated = accumulated * decay[..., None] + jnp.einsum(
                "uaco,ouw->uacw",
                weights.astype(jnp.bfloat16),
                values_here,
                preferred_element_type=jnp.float32,
            )
            return (new_running, denominator, accumulated)

        return lax.cond(key_start > last_query, lambda current: current, compute, inner)

    running, denominator, accumulated = lax.fori_loop(0, turns, one_block, initial)
    attended = (accumulated / denominator[..., None]).transpose(2, 0, 1, 3)
    attended = attended.reshape(block_rows, local_heads * head_dim).astype(jnp.bfloat16)
    partial_sums = jnp.dot(
        attended,
        lax.all_gather(out_weight, "ctx", axis=1, tiled=True),
        preferred_element_type=jnp.float32,
    )
    head_total = lax.psum_scatter(
        partial_sums.astype(jnp.bfloat16), "exp", scatter_dimension=0, tiled=True
    ).astype(jnp.float32)
    mixed = (tokens.astype(jnp.float32) + head_total).astype(jnp.bfloat16)
    moe_in = normed(mixed, moe_gain).astype(jnp.bfloat16)
    top_count = expert_ids.shape[1]
    expert_count = exp_count * gate_weight.shape[0]
    capacity = min(tok_rows, 2 * tok_rows * top_count // expert_count)
    flattened_expert_index = expert_ids.reshape(-1)
    one_hot = (
        flattened_expert_index[:, None] == jnp.arange(expert_count, dtype=jnp.int32)[None, :]
    ).astype(jnp.int32)
    earlier = jnp.cumsum(one_hot, axis=0) - one_hot
    slot_rank = jnp.sum(earlier * one_hot, axis=1)
    slot_index = flattened_expert_index * capacity + slot_rank
    slot_grid = slot_index.reshape(tok_rows, top_count)
    selection = jnp.any(
        jnp.arange(expert_count * capacity, dtype=jnp.int32)[:, None, None] == slot_grid[None],
        axis=-1,
    )
    send_rows = jnp.dot(
        selection.astype(jnp.bfloat16), moe_in, preferred_element_type=jnp.float32
    ).astype(jnp.bfloat16)
    send_rows = send_rows.reshape(expert_count, capacity, width)
    codes = route_code.astype(jnp.float32)
    route_weight = codes / jnp.sum(codes, axis=-1, keepdims=True)
    arrived = lax.all_to_all(send_rows, "exp", split_axis=0, concat_axis=0, tiled=True)
    flat_rows = arrived.reshape(-1, width)
    gate_sums = jnp.dot(flat_rows, gate_weight[0], preferred_element_type=jnp.float32)
    up_sums = jnp.dot(flat_rows, up_weight[0], preferred_element_type=jnp.float32)
    hidden_state = (jax.nn.silu(gate_sums) * up_sums).astype(jnp.bfloat16)
    expert_out = jnp.dot(
        hidden_state, expert_down_matrix[0], preferred_element_type=jnp.float32
    ).astype(jnp.bfloat16)
    gathered_back = lax.all_to_all(
        expert_out.reshape(arrived.shape), "exp", split_axis=0, concat_axis=0, tiled=True
    )
    flat_back = gathered_back.reshape(expert_count * capacity, width)
    picked = (
        jnp.take(flat_back, slot_index, axis=0)
        .astype(jnp.float32)
        .reshape(tok_rows, top_count, width)
    )
    expert_sum = jnp.sum(picked * route_weight[..., None], axis=1)
    return (mixed.astype(jnp.float32) + expert_sum).astype(jnp.bfloat16)


def solution(mesh):
    placed = (
        P(("ctx", "exp"), None),
        P(),
        P("ctx", "exp"),
        P("ctx", None),
        P("ctx", None),
        P(),
        P(),
        P("exp", "ctx"),
        P(),
        P(("ctx", "exp"), None),
        P(("ctx", "exp"), None),
        P("exp", None, None),
        P("exp", None, None),
        P("exp", None, None),
    )
    return jax.shard_map(
        shards, mesh=mesh, in_specs=placed, out_specs=P(("ctx", "exp"), None), check_vma=False
    )
```

profile of v0, /device:TPU:8, one launch (start us, length us, event | category | flops | bytes accessed | tf_op | source)
XLA Modules:
  0.0 891.4 jit_solution(7393212697054446029)
XLA Ops:
  13.2 76.4 %all-gather.7.cloned.1.call-done = bf16[512,2048]{1,0:T(8,128)(2,1)} async-done(((bf16[64,2048]{1,0:T(8,128)(2,1)}), bf16[512,2048]{1,0:T(8,128)(2,1)}) %all-gather.7.cloned.1.call-update) | async-done | bytes 2097168 | tf_op jit(solution)/shard_map/all_gather | solution.py:46
  89.6 57.4 %all-gather.9.cloned.1.call-done = bf16[2048,512]{1,0:T(8,128)(2,1)} async-done(((bf16[64,512]{1,0:T(8,128)(2,1)}), bf16[2048,512]{1,0:T(8,128)(2,1)}) %all-gather.9.cloned.1.call-update) | async-done | bytes 2097168 | tf_op jit(solution)/shard_map/all_gather | solution.py:49
  149.7 58.3 %all-gather.11.cloned.1.call-done = bf16[2048,512]{1,0:T(8,128)(2,1)} async-done(((bf16[64,512]{1,0:T(8,128)(2,1)}), bf16[2048,512]{1,0:T(8,128)(2,1)}) %all-gather.11.cloned.1.call-update) | async-done | bytes 2097168 | tf_op jit(solution)/shard_map/all_gather | solution.py:50
  212.6 56.2 %all-gather.15.cloned.1.call-done = bf16[2048,512]{1,0:T(8,128)(2,1)} async-done(((bf16[64,512]{1,0:T(8,128)(2,1)}), bf16[2048,512]{1,0:T(8,128)(2,1)}) %all-gather.15.cloned.1.call-update) | async-done | bytes 2097168 | tf_op jit(solution)/shard_map/all_gather | solution.py:48
  268.7 4.5 bitcast_reduce_fusion
  278.2 60.8 %all-gather.13.cloned.1.call-done = bf16[16384,256]{0,1:T(8,128)(2,1)} async-done(((bf16[512,256]{0,1:T(8,128)(2,1)}), bf16[16384,256]{0,1:T(8,128)(2,1)}) %all-gather.13.cloned.1.call-update) | async-done | bytes 8388624 | tf_op jit(solution)/shard_map/all_gather | solution.py:70
  339.0 11.9 %copy.38 = bf16[16384,256]{1,0:T(8,128)(2,1)} copy(bf16[16384,256]{0,1:T(8,128)(2,1)} %all-gather.13.cloned.1.call-done) | data formatting | bytes 16777216
  352.0 118.2 %while.18 = (s32[]{:T(128)}, f32[1,4,512]{2,1,0:T(4,128)S(1)}, f32[1,4,512]{2,1,0:T(4,128)S(1)}, f32[1,4,512,128]{3,2,1,0:T(8,128)}, s32[]{:T(128)}, /*index=5*/...) while((s32[]{:T(128)}, f32[1,4,512]{2,1,0:T(4,128)S(1)}, ...), condition=%wide.region_9.10_spmd.clone, body=%wide.region_4.9_spmd.clone.sunk | while | flops 551296000 | bytes 33436000 | solution.py:109
  352.7 10.5 %conditional.3 = (f32[1,4,512]{2,1,0:T(4,128)S(1)}, f32[1,4,512]{2,1,0:T(4,128)S(1)}, f32[1,4,512,128]{3,2,1,0:T(8,128)}) conditional(s32[]{:T(128)} %convert_element_type.184, (s32[]{:T(128)}, s32[]{:T(128)}, s32[]{:T(128)}, bf16[16384,256]{1,0:T(8,128)(2,1)}, bf16[512,1,4,128]{3,0,2,1:T(8,128)(2,1)}, /*index=5*/f32[1,4,512]{2,1,0:T(4,128)S(1)}, ...), branch_computations={%region_5.7_spmd, %region_8.8_spmd} | conditional | flops 551296000 | bytes 33417346 | solution.py:107
  356.9 5.2 fusion.12
  364.0 10.5 %conditional.3 = (f32[1,4,512]{2,1,0:T(4,128)S(1)}, f32[1,4,512]{2,1,0:T(4,128)S(1)}, f32[1,4,512,128]{3,2,1,0:T(8,128)}) conditional(s32[]{:T(128)} %convert_element_type.184, (s32[]{:T(128)}, s32[]{:T(128)}, s32[]{:T(128)}, bf16[16384,256]{1,0:T(8,128)(2,1)}, bf16[512,1,4,128]{3,0,2,1:T(8,128)(2,1)}, /*index=5*/f32[1,4,512]{2,1,0:T(4,128)S(1)}, ...), branch_computations={%region_5.7_spmd, %region_8.8_spmd} | conditional | flops 551296000 | bytes 33417346 | solution.py:107
  368.2 5.2 fusion.12
  375.2 10.5 %conditional.3 = (f32[1,4,512]{2,1,0:T(4,128)S(1)}, f32[1,4,512]{2,1,0:T(4,128)S(1)}, f32[1,4,512,128]{3,2,1,0:T(8,128)}) conditional(s32[]{:T(128)} %convert_element_type.184, (s32[]{:T(128)}, s32[]{:T(128)}, s32[]{:T(128)}, bf16[16384,256]{1,0:T(8,128)(2,1)}, bf16[512,1,4,128]{3,0,2,1:T(8,128)(2,1)}, /*index=5*/f32[1,4,512]{2,1,0:T(4,128)S(1)}, ...), branch_computations={%region_5.7_spmd, %region_8.8_spmd} | conditional | flops 551296000 | bytes 33417346 | solution.py:107
  379.4 5.2 fusion.12
  386.4 10.5 %conditional.3 = (f32[1,4,512]{2,1,0:T(4,128)S(1)}, f32[1,4,512]{2,1,0:T(4,128)S(1)}, f32[1,4,512,128]{3,2,1,0:T(8,128)}) conditional(s32[]{:T(128)} %convert_element_type.184, (s32[]{:T(128)}, s32[]{:T(128)}, s32[]{:T(128)}, bf16[16384,256]{1,0:T(8,128)(2,1)}, bf16[512,1,4,128]{3,0,2,1:T(8,128)(2,1)}, /*index=5*/f32[1,4,512]{2,1,0:T(4,128)S(1)}, ...), branch_computations={%region_5.7_spmd, %region_8.8_spmd} | conditional | flops 551296000 | bytes 33417346 | solution.py:107
  390.6 5.2 fusion.12
  397.6 10.5 %conditional.3 = (f32[1,4,512]{2,1,0:T(4,128)S(1)}, f32[1,4,512]{2,1,0:T(4,128)S(1)}, f32[1,4,512,128]{3,2,1,0:T(8,128)}) conditional(s32[]{:T(128)} %convert_element_type.184, (s32[]{:T(128)}, s32[]{:T(128)}, s32[]{:T(128)}, bf16[16384,256]{1,0:T(8,128)(2,1)}, bf16[512,1,4,128]{3,0,2,1:T(8,128)(2,1)}, /*index=5*/f32[1,4,512]{2,1,0:T(4,128)S(1)}, ...), branch_computations={%region_5.7_spmd, %region_8.8_spmd} | conditional | flops 551296000 | bytes 33417346 | solution.py:107
  401.8 5.2 fusion.12
  408.8 10.5 %conditional.3 = (f32[1,4,512]{2,1,0:T(4,128)S(1)}, f32[1,4,512]{2,1,0:T(4,128)S(1)}, f32[1,4,512,128]{3,2,1,0:T(8,128)}) conditional(s32[]{:T(128)} %convert_element_type.184, (s32[]{:T(128)}, s32[]{:T(128)}, s32[]{:T(128)}, bf16[16384,256]{1,0:T(8,128)(2,1)}, bf16[512,1,4,128]{3,0,2,1:T(8,128)(2,1)}, /*index=5*/f32[1,4,512]{2,1,0:T(4,128)S(1)}, ...), branch_computations={%region_5.7_spmd, %region_8.8_spmd} | conditional | flops 551296000 | bytes 33417346 | solution.py:107
  413.0 5.2 fusion.12
  420.0 10.5 %conditional.3 = (f32[1,4,512]{2,1,0:T(4,128)S(1)}, f32[1,4,512]{2,1,0:T(4,128)S(1)}, f32[1,4,512,128]{3,2,1,0:T(8,128)}) conditional(s32[]{:T(128)} %convert_element_type.184, (s32[]{:T(128)}, s32[]{:T(128)}, s32[]{:T(128)}, bf16[16384,256]{1,0:T(8,128)(2,1)}, bf16[512,1,4,128]{3,0,2,1:T(8,128)(2,1)}, /*index=5*/f32[1,4,512]{2,1,0:T(4,128)S(1)}, ...), branch_computations={%region_5.7_spmd, %region_8.8_spmd} | conditional | flops 551296000 | bytes 33417346 | solution.py:107
  424.2 5.2 fusion.12
  431.2 10.5 %conditional.3 = (f32[1,4,512]{2,1,0:T(4,128)S(1)}, f32[1,4,512]{2,1,0:T(4,128)S(1)}, f32[1,4,512,128]{3,2,1,0:T(8,128)}) conditional(s32[]{:T(128)} %convert_element_type.184, (s32[]{:T(128)}, s32[]{:T(128)}, s32[]{:T(128)}, bf16[16384,256]{1,0:T(8,128)(2,1)}, bf16[512,1,4,128]{3,0,2,1:T(8,128)(2,1)}, /*index=5*/f32[1,4,512]{2,1,0:T(4,128)S(1)}, ...), branch_computations={%region_5.7_spmd, %region_8.8_spmd} | conditional | flops 551296000 | bytes 33417346 | solution.py:107
  435.4 5.2 fusion.12
  442.4 10.5 %conditional.3 = (f32[1,4,512]{2,1,0:T(4,128)S(1)}, f32[1,4,512]{2,1,0:T(4,128)S(1)}, f32[1,4,512,128]{3,2,1,0:T(8,128)}) conditional(s32[]{:T(128)} %convert_element_type.184, (s32[]{:T(128)}, s32[]{:T(128)}, s32[]{:T(128)}, bf16[16384,256]{1,0:T(8,128)(2,1)}, bf16[512,1,4,128]{3,0,2,1:T(8,128)(2,1)}, /*index=5*/f32[1,4,512]{2,1,0:T(4,128)S(1)}, ...), branch_computations={%region_5.7_spmd, %region_8.8_spmd} | conditional | flops 551296000 | bytes 33417346 | solution.py:107
  446.6 5.2 fusion.12
  474.9 4.4 convolution_convert_fusion
  480.4 331.5 %reduce-scatter.2.cloned.1.call-done = bf16[64,2048]{1,0:T(8,128)(2,1)} async-done(((bf16[512,2048]{1,0:T(8,128)(2,1)}), bf16[64,2048]{1,0:T(8,128)(2,1)}) %reduce-scatter.2.cloned.1.call-update) | async-done | bytes 262160 | tf_op jit(solution)/shard_map/reduce_scatter | solution.py:117
  814.7 30.4 %all_to_all.10 = bf16[8,32,2048]{2,1,0:T(8,128)(2,1)S(1)} all-to-all(bf16[8,32,2048]{2,1,0:T(8,128)(2,1)S(1)} %bitcast.94), channel_id=1, replica_groups=mesh['ctx'=32,'exp'=8] {'exp'}, dimensions={0} | all-to-all | bytes 2097152 | tf_op jit(solution)/shard_map/all_to_all | solution.py:143
  847.9 5.5 fusion.28
  853.4 4.2 all-to-all-start.1
  858.2 15.4 %all-to-all-done.1 = bf16[8,32,2048]{2,1,0:T(8,128)(2,1)} async-done(((bf16[8,32,2048]{2,1,0:T(8,128)(2,1)}), bf16[8,32,2048]{2,1,0:T(8,128)(2,1)}, u32[]{:S(2)}, u32[]{:S(2)}) %all-to-all-start.1) | async-done | bytes 1048608 | tf_op jit(solution)/shard_map/all_to_all | solution.py:151
  (260 shorter events, 90.5 us)
Async XLA Ops:
  6.5 841.4 %copy-start = (bf16[1,768,2048]{2,1,0:T(8,128)(2,1)S(1)}, bf16[1,768,2048]{2,1,0:T(8,128)(2,1)}, u32[]{:S(2)}) copy-start(bf16[1,768,2048]{2,1,0:T(8,128)(2,1)} %param.31) | copy-start | bytes 9437188
  6.5 83.1 %all-gather.7.cloned.1.call-start = ((), (), s32[]{:S(2)}) async-start(), calls=%async_computation.3 | async-start | bytes 2359296 | tf_op jit(solution)/shard_map/all_gather | solution.py:46
  10.4 136.6 %all-gather.9.cloned.1.call-start = ((), (), s32[]{:S(2)}) async-start(), calls=%async_computation.4 | async-start | bytes 2162688 | tf_op jit(solution)/shard_map/all_gather | solution.py:49
  11.2 196.8 %all-gather.11.cloned.1.call-start = ((), (), s32[]{:S(2)}) async-start(), calls=%async_computation.5 | async-start | bytes 2162688 | tf_op jit(solution)/shard_map/all_gather | solution.py:50
  11.9 256.8 %all-gather.15.cloned.1.call-start = ((), (), s32[]{:S(2)}) async-start(), calls=%async_computation.7 | async-start | bytes 2162688 | tf_op jit(solution)/shard_map/all_gather | solution.py:48
  12.5 326.5 %all-gather.13.cloned.1.call-start = ((), (), s32[]{:S(2)}) async-start(), calls=%async_computation.6 | async-start | bytes 8650752 | tf_op jit(solution)/shard_map/all_gather | solution.py:70
  13.2 198.6 %copy-start.8 = (bf16[128]{0:T(256)(128)(2,1)S(1)}, bf16[128]{0:T(256)(128)(2,1)}, u32[]{:S(2)}) copy-start(bf16[128]{0:T(256)(128)(2,1)} %param.23) | copy-start | bytes 772
  211.2 263.7 %all-gather.17.cloned.1.call-start = ((), (), s32[]{:S(2)}) async-start(), calls=%async_computation.8 | async-start | bytes 2162688 | tf_op jit(solution)/shard_map/all_gather | solution.py:114
  211.8 600.1 %reduce-scatter.2.cloned.1.call-start = ((), (), s32[]{:S(2)}) async-start(), calls=%async_computation.9 | async-start | bytes 2359296 | tf_op jit(solution)/shard_map/reduce_scatter | solution.py:117
  356.9 5.2 copy-start.1
  368.2 5.2 copy-start.1
  379.4 5.3 copy-start.1
  390.6 5.3 copy-start.1
  401.8 5.2 copy-start.1
  413.0 5.2 copy-start.1
  424.2 5.2 copy-start.1
  435.4 5.2 copy-start.1
  446.6 5.2 copy-start.1
  474.9 4.5 copy-start.4
  474.9 5.4 copy-start.5
  474.9 337.0 %copy-start.2 = (bf16[64,2048]{1,0:T(8,128)(2,1)S(1)}, bf16[64,2048]{1,0:T(8,128)(2,1)}, u32[]{:S(2)}) copy-start(bf16[64,2048]{1,0:T(8,128)(2,1)} %param.18) | copy-start | bytes 786436
  811.9 34.2 %copy-start.7 = (bf16[1,2048,768]{2,1,0:T(8,128)(2,1)S(1)}, bf16[1,2048,768]{2,1,0:T(8,128)(2,1)}, u32[]{:S(2)}) copy-start(bf16[1,2048,768]{2,1,0:T(8,128)(2,1)} %param.29) | copy-start | bytes 9437188
  845.0 1.0 copy-start.3
  847.9 10.1 %copy-start.6 = (s32[64,2]{0,1:T(2,128)S(1)}, s32[64,2]{0,1:T(2,128)}, u32[]{:S(2)}) copy-start(s32[64,2]{0,1:T(2,128)} %param.28) | copy-start | bytes 1540
  853.4 20.2 %all-to-all-start.1 = ((bf16[8,32,2048]{2,1,0:T(8,128)(2,1)}), bf16[8,32,2048]{2,1,0:T(8,128)(2,1)}, u32[]{:S(2)}, u32[]{:S(2)}) async-start(bf16[8,32,2048]{2,1,0:T(8,128)(2,1)} %bitcast.97), calls=%async_computation.2 | async-start | bytes 2097152 | tf_op jit(solution)/shard_map/all_to_all | solution.py:151
Sparse Core Ops, SparseCore 0:
  10.5 79.0 all-gather.6
  91.5 55.5 all-gather.8
  148.9 59.0 all-gather.10
  209.7 59.0 all-gather.14
  270.5 68.4 all-gather.12
  340.7 58.4 all-gather.16
  479.5 332.3 reduce-scatter.1
where the time goes:
time: 901 us; the launch traced here: 891 us
  waiting for transfers between devices  658 us (73%)
  matrix products  105 us (12%)
  blocking collectives  30.4 us (3%)
  other arithmetic  29.3 us (3%)
  local copies, waits for them, and re-layouts  26.1 us (3%)
  loops' own time  24 us (3%)
  between operations  13.7 us (2%)
    reduce_scatter x1, waiting for transfers between devices, shards(): lax.psum_scatter(partial_sums.astype(jnp.bfloat16), 'exp', scatter_dimens...  331 us
    all_gather x1, waiting for transfers between devices, shards(): block_tokens = lax.all_gather(normal_rows, 'exp', axis=0, tiled=True)  76.4 us
    all_gather x1, waiting for transfers between devices, shards(): pieces = lax.all_gather(travelling, 'ctx', axis=0, tiled=True)  60.8 us
    all_gather x1, waiting for transfers between devices, shards(): lax.all_gather(v_weight, 'ctx', axis=0, tiled=True)  58.3 us
    all_gather x1, waiting for transfers between devices, shards(): lax.all_gather(k_weight, 'ctx', axis=0, tiled=True)  57.4 us
    all_gather x1, waiting for transfers between devices, shards(): lax.all_gather(q_weight, 'ctx', axis=0, tiled=True)  56.2 us
    dot_general x9, matrix products, compute(): jnp.einsum('uaco,ouw->uacw', weights.astype(jnp.bfloat16), values_here, p...  46.9 us
    dot_general x9, matrix products, compute(): jnp.einsum('azpw,czw->zpac', grouped_query_rows, resident_key_block, pref...  35.3 us
  transfers between devices with their start and end apart: 8, of which 7 were waited for; matrix products, arithmetic and copies ran while one was open for 15% of the time, Pallas kernels for 0%

commit v1 on v0

v1 whole, which is shorter than its diff:
```python
import functools
import math

import jax
import jax.numpy as jnp
from jax import lax
from jax.experimental import pallas as pl
from jax.experimental.pallas import tpu as pltpu
from jax.sharding import PartitionSpec as P

F32 = jnp.float32
BF16 = jnp.bfloat16
NT = (((1,), (1,)), ((), ()))
EPS = 1e-06


def normed(values, gain):
    widened = values.astype(F32)
    square = jnp.mean(widened * widened, axis=-1, keepdims=True)
    return widened * lax.rsqrt(square + EPS) * gain.astype(F32)


def params(vmem_mib):
    return pltpu.CompilerParams(vmem_limit_bytes=vmem_mib * 2**20)


def kv_kernel(place_ref, own_ref, other_ref, w_ref, gain_ref, out_ref):
    half, head = own_ref.shape[0], gain_ref.shape[1]
    mine = place_ref[0]
    for rows_ref, spot in ((own_ref, mine), (other_ref, 1 - mine)):
        sums = jnp.dot(rows_ref[...], w_ref[...], preferred_element_type=F32)
        keys = normed(sums[:, :head], gain_ref[...]).astype(BF16)
        start = pl.multiple_of(spot * half, half)
        out_ref[pl.ds(start, half), :head] = keys
        for part in range(half // head):
            block = sums[part * head : (part + 1) * head, head:]
            out_ref[pl.ds(pl.multiple_of(start + part * head, head), head), head:] = block.T.astype(
                BF16
            )


def q_kernel(place_ref, own_ref, other_ref, w_ref, gain_ref, out_ref):
    head = gain_ref.shape[1]
    mine = place_ref[0]
    for rows_ref, spot in ((own_ref, mine), (other_ref, 1 - mine)):
        sums = jnp.dot(rows_ref[...], w_ref[...], preferred_element_type=F32)
        for one in range(w_ref.shape[1] // head):
            cols = slice(one * head, (one + 1) * head)
            out_ref[spot, :, cols] = normed(sums[:, cols], gain_ref[...]).astype(BF16)


def project(kernel, place, own, other, weights, col_block, width, gain, out_shape):
    half, depth = own.shape
    return pl.pallas_call(
        kernel,
        grid_spec=pltpu.PrefetchScalarGridSpec(
            num_scalar_prefetch=1,
            grid=(1,),
            in_specs=[
                pl.BlockSpec((half, depth), lambda i, p: (0, 0)),
                pl.BlockSpec((half, depth), lambda i, p: (0, 0)),
                pl.BlockSpec((depth, width), lambda i, p: (0, col_block)),
                pl.BlockSpec((1, gain.shape[0]), lambda i, p: (0, 0)),
            ],
            out_specs=pl.BlockSpec(out_shape, lambda i, p: (0,) * len(out_shape)),
        ),
        out_shape=jax.ShapeDtypeStruct(out_shape, BF16),
        compiler_params=params(40),
        cost_estimate=pl.CostEstimate(
            flops=4 * half * depth * width, bytes_accessed=8 * 2**20, transcendentals=0
        ),
    )(place, own, other, weights, gain.reshape(1, -1))


def attention_kernel(scale, place_ref, qa_ref, qb_ref, kv_ref, wo_ref, out_ref, acc_ref, att_ref):
    rows, feats = qa_ref.shape
    head = acc_ref.shape[1]
    heads = feats // head
    block = 2 * rows
    ctx = kv_ref.shape[0] // block
    place = place_ref[0]

    def keys_at(start, count):
        part = kv_ref[pl.ds(pl.multiple_of(start, rows), count), :]
        values = jnp.concatenate(
            [part[i * head : (i + 1) * head, head:] for i in range(count // head)], axis=1
        )
        return part[:, :head], values

    for job, q_ref in ((0, qa_ref), (1, qb_ref)):
        blocks = place if job == 0 else ctx - 1 - place

        def step(start, count, state, first=False, q_ref=q_ref):
            keys, values = keys_at(start, count)
            fresh = []
            for one in range(heads):
                scores = lax.dot_general(
                    keys, q_ref[:, one * head : (one + 1) * head], NT, preferred_element_type=F32
                )
                if first:
                    key_at = lax.broadcasted_iota(jnp.int32, scores.shape, 0)
                    row_at = lax.broadcasted_iota(jnp.int32, scores.shape, 1)
                    scores = jnp.where(key_at <= row_at, scores, -1e30)
                largest = jnp.max(scores, axis=0, keepdims=True)
                if not first:
                    largest = jnp.maximum(largest, state[2 * one])
                weights = jnp.exp2((scores - largest) * scale)
                partial = jnp.sum(weights.reshape(count // 8, 8, rows), axis=0)
                product = lax.dot_general(
                    values,
                    weights.astype(BF16),
                    (((1,), (0,)), ((), ())),
                    preferred_element_type=F32,
                )
                if first:
                    acc_ref[one] = product
                else:
                    decay = jnp.exp2((state[2 * one] - largest) * scale)
                    partial = state[2 * one + 1] * decay + partial
                    acc_ref[one] = acc_ref[one] * decay + product
                fresh += [largest, partial]
            return tuple(fresh)

        state = step(blocks * block + job * rows, rows, None, first=True)
        if job == 1:
            state = step(blocks * block, rows, state)
        state = lax.fori_loop(0, blocks, lambda i, now: step(i * block, block, now), state)
        for one in range(heads):
            total = jnp.sum(state[2 * one + 1], axis=0, keepdims=True)
            att_ref[:, one * head : (one + 1) * head] = (acc_ref[one] / total).T.astype(BF16)
        width = wo_ref.shape[0]
        piece = min(512, width)
        for at in range(0, width, piece):
            out_ref[job, :, at : at + piece] = lax.dot_general(
                att_ref[...], wo_ref[at : at + piece, :], NT, preferred_element_type=F32
            ).astype(BF16)


def attend(place, q_a, q_b, kv, weights, head):
    rows, feats = q_a.shape
    width = weights.shape[0]
    whole = lambda i, p: (0, 0)
    flops = 8 * kv.shape[0] * rows * feats
    return pl.pallas_call(
        functools.partial(attention_kernel, math.log2(math.e) / math.sqrt(head)),
        grid_spec=pltpu.PrefetchScalarGridSpec(
            num_scalar_prefetch=1,
            grid=(1,),
            in_specs=[
                pl.BlockSpec((rows, feats), whole),
                pl.BlockSpec((rows, feats), whole),
                pl.BlockSpec(kv.shape, whole, pipeline_mode=pl.Buffered(1)),
                pl.BlockSpec((width, feats), lambda i, p: (0, 1), pipeline_mode=pl.Buffered(1)),
            ],
            out_specs=pl.BlockSpec((2, rows, width), lambda i, p: (0, 0, 0)),
            scratch_shapes=[
                pltpu.VMEM((feats // head, head, rows), F32),
                pltpu.VMEM((rows, feats), BF16),
            ],
        ),
        out_shape=jax.ShapeDtypeStruct((2, rows, width), BF16),
        compiler_params=params(48),
        cost_estimate=pl.CostEstimate(
            flops=flops, bytes_accessed=16 * 2**20, transcendentals=flops // 256
        ),
    )(place, q_a, q_b, kv, weights)


def shards(
    tokens,
    attn_gain,
    q_weight,
    k_weight,
    v_weight,
    q_gain,
    k_gain,
    out_weight,
    moe_gain,
    expert_ids,
    route_code,
    gate_weight,
    up_weight,
    expert_down_matrix,
):
    exp_count = lax.axis_size("exp")
    ctx_count = lax.axis_size("ctx")
    ctx_place = lax.axis_index("ctx")
    exp_place = lax.axis_index("exp")
    tok_rows, width = tokens.shape
    head = q_gain.shape[0]
    feats = q_weight.shape[1]
    group_size = feats * exp_count // k_weight.shape[1]
    kv_first = exp_place * (feats // head) // group_size * head
    ring = exp_count // 2
    half_rows = tok_rows * ring
    far = exp_place // ring
    near = exp_place % ring
    rings = [list(range(ring)), list(range(ring, exp_count))]
    flip = [(e, (e + ring) % exp_count) for e in range(exp_count)]
    mirror = [(c, ctx_count - 1 - c) for c in range(ctx_count)]

    def over_ring(parts):
        return lax.all_to_all(parts, "exp", 0, 0, tiled=True, axis_index_groups=rings)

    def to_ring(rows):
        spread = jnp.broadcast_to(rows[None], (ring,) + rows.shape)
        return over_ring(spread).reshape(half_rows, width)

    packed = jnp.concatenate(
        [
            q_weight,
            out_weight.T,
            lax.dynamic_slice_in_dim(k_weight, kv_first, head, 1),
            lax.dynamic_slice_in_dim(v_weight, kv_first, head, 1),
        ],
        axis=1,
    )
    weights = lax.all_gather(packed, "ctx", axis=0, tiled=True)
    normal_rows = normed(tokens, attn_gain).astype(BF16)
    flipped = lax.ppermute(normal_rows, "exp", flip)
    own = to_ring(normal_rows)
    other = to_ring(flipped)
    far_index = far.astype(jnp.int32).reshape(1)
    kv = project(
        kv_kernel,
        far_index,
        own,
        other,
        weights,
        feats // head,
        2 * head,
        k_gain,
        (2 * half_rows, 2 * head),
    )
    kv_all = lax.all_gather(kv, "ctx", axis=0, tiled=True)
    queries = project(
        q_kernel, far_index, own, other, weights, 0, feats, q_gain, (2, half_rows, feats)
    )
    mirrored = lax.ppermute(queries[1], "ctx", mirror)
    sums = attend(
        ctx_place.astype(jnp.int32).reshape(1), queries[0], mirrored, kv_all, weights, head
    )
    parts = sums.reshape(2, ring, tok_rows, width).swapaxes(0, 1)
    shares = jnp.sum(over_ring(parts).astype(F32), axis=0)
    rounded = shares.astype(BF16)
    near_half, far_half = range(ring), range(ring, exp_count)
    by_flip = lax.ppermute(rounded[0], "exp", [(e, e - ring) for e in far_half])
    cross = [(c * exp_count + e, (ctx_count - 1 - c) * exp_count + e + ring)
             for c in range(ctx_count) for e in near_half]
    straight = [(c * exp_count + e, (ctx_count - 1 - c) * exp_count + e)
                for c in range(ctx_count) for e in far_half]
    by_cross = lax.ppermute(rounded[1], ("ctx", "exp"), cross)
    by_mirror = lax.ppermute(rounded[1], ("ctx", "exp"), straight)
    head_total = jnp.where(
        far == 0,
        shares[0] + by_flip.astype(F32),
        by_mirror.astype(F32) + by_cross.astype(F32),
    )
    mixed = (tokens.astype(F32) + head_total).astype(BF16)
    moe_in = normed(mixed, moe_gain).astype(BF16)
    top_count = expert_ids.shape[1]
    expert_count = exp_count * gate_weight.shape[0]
    capacity = min(tok_rows, 2 * tok_rows * top_count // expert_count)
    flat_ids = expert_ids.reshape(-1)
    one_hot = (flat_ids[:, None] == jnp.arange(expert_count, dtype=jnp.int32)[None, :]).astype(
        jnp.int32
    )
    earlier = jnp.cumsum(one_hot, axis=0) - one_hot
    slot_rank = jnp.sum(earlier * one_hot, axis=1)
    slots = (flat_ids * capacity + slot_rank).reshape(tok_rows, top_count)
    places = jnp.arange(expert_count * capacity, dtype=jnp.int32)
    selection = jnp.any(places[:, None, None] == slots[None], axis=-1)
    send_rows = jnp.dot(selection.astype(BF16), moe_in, preferred_element_type=F32).astype(BF16)
    send_rows = send_rows.reshape(expert_count, capacity, width)
    codes = route_code.astype(F32)
    route_weight = codes / jnp.sum(codes, axis=-1, keepdims=True)
    arrived = lax.all_to_all(send_rows, "exp", split_axis=0, concat_axis=0, tiled=True)
    flat_rows = arrived.reshape(-1, width)
    gate_sums = jnp.dot(flat_rows, gate_weight[0], preferred_element_type=F32)
    up_sums = jnp.dot(flat_rows, up_weight[0], preferred_element_type=F32)
    hidden = (jax.nn.silu(gate_sums) * up_sums).astype(BF16)
    expert_out = jnp.dot(hidden, expert_down_matrix[0], preferred_element_type=F32).astype(BF16)
    back = lax.all_to_all(
        expert_out.reshape(arrived.shape), "exp", split_axis=0, concat_axis=0, tiled=True
    ).reshape(expert_count * capacity, width)
    total = mixed.astype(F32)
    for j in range(top_count):
        pick = (slots[:, j : j + 1] == places[None, :]).astype(BF16)
        picked = jnp.dot(pick, back, preferred_element_type=F32)
        total = total + picked * route_weight[:, j : j + 1]
    return total.astype(BF16)


def solution(mesh):
    placed = (
        P(("ctx", "exp"), None),
        P(),
        P("ctx", "exp"),
        P("ctx", None),
        P("ctx", None),
        P(),
        P(),
        P("exp", "ctx"),
        P(),
        P(("ctx", "exp"), None),
        P(("ctx", "exp"), None),
        P("exp", None, None),
        P("exp", None, None),
        P("exp", None, None),
    )
    return jax.shard_map(
        shards, mesh=mesh, in_specs=placed, out_specs=P(("ctx", "exp"), None), check_vma=False
    )
```

time: 901 us -> 373 us (0.41)
  the two profiles are of different devices: /device:TPU:8 before, /device:TPU:65 now
where the time goes in v1:
time: 373 us; the launch traced here: 372 us
  waiting for transfers between devices  183 us (49%)
  Pallas kernels  71.5 us (19%)
  blocking collectives  36.1 us (10%)
  starting transfers between devices  34.7 us (9%)
  between operations  13.7 us (4%)
  local copies, waits for them, and re-layouts  12.8 us (3%)
  matrix products  11.7 us (3%)
  other arithmetic  8.48 us (2%)
    pallas_call x1, Pallas kernels, attend(): pl.pallas_call(functools.partial(attention_kernel, math.log2(math.e) / ma...  65.4 us
    all_gather x1, waiting for transfers between devices, shards(): kv_all = lax.all_gather(kv, 'ctx', axis=0, tiled=True)  50.5 us
    all_to_all x3, waiting for transfers between devices, over_ring(): lax.all_to_all(parts, 'exp', 0, 0, tiled=True, axis_index_groups=rings)  37.4 us
    all_to_all x1, blocking collectives, shards(): lax.all_to_all(send_rows, 'exp', split_axis=0, concat_axis=0, tiled=True)  36.1 us
    all_gather x1, waiting for transfers between devices, shards(): weights = lax.all_gather(packed, 'ctx', axis=0, tiled=True)  26.9 us
    all_to_all x1, waiting for transfers between devices, shards(): lax.all_to_all(expert_out.reshape(arrived.shape), 'exp', split_axis=0, co...  23.1 us
    ppermute x1, waiting for transfers between devices, shards(): flipped = lax.ppermute(normal_rows, 'exp', flip)  16.2 us
    ppermute x1, waiting for transfers between devices, shards(): mirrored = lax.ppermute(queries[1], 'ctx', mirror)  15.9 us
  transfers between devices with their start and end apart: 11, of which 8 were waited for; matrix products, arithmetic and copies ran while one was open for 2% of the time, Pallas kernels for 1%

profile of v1, /device:TPU:65, one launch (start us, length us, event | category | flops | bytes accessed | tf_op | source)
XLA Modules:
  0.0 372.4 jit_solution(789128853297927080)
XLA Ops:
  7.4 1.6 pad_maximum_fusion
  12.0 1.1 broadcast_in_dim.4
  13.1 4.2 %all-to-all-start = ((bf16[4,64,2048]{2,1,0:T(8,128)(2,1)}), bf16[4,64,2048]{2,1,0:T(8,128)(2,1)}, u32[]{:S(2)}, u32[]{:S(2)}) async-start(bf16[4,64,2048]{2,1,0:T(8,128)(2,1)} %broadcast_in_dim.4), calls=%async_computation | async-start | bytes 2097152 | tf_op jit(solution)/shard_map/all_to_all | solution.py:203
  17.4 5.2 %collective-permute-start = (bf16[64,2048]{1,0:T(8,128)(2,1)S(1)}, bf16[64,2048]{1,0:T(8,128)(2,1)}, u32[]{:S(2)}, u32[]{:S(2)}) collective-permute-start(bf16[64,2048]{1,0:T(8,128)(2,1)S(1)} %fusion.22), channel_id=1, source_target_pairs={{0,4},{1,5},{2,6},{3,7},{4,0},{5,1},{6,2},{7,3},{8,12},{9,13},{10,... | collective-permute-start | bytes 786440 | tf_op jit(solution)/shard_map/ppermute | solution.py:220
  22.6 16.2 %collective-permute-done = bf16[64,2048]{1,0:T(8,128)(2,1)} collective-permute-done((bf16[64,2048]{1,0:T(8,128)(2,1)S(1)}, bf16[64,2048]{1,0:T(8,128)(2,1)}, u32[]{:S(2)}, u32[]{:S(2)}) %collective-permute-start) | collective-permute-done | bytes 262176 | tf_op jit(solution)/shard_map/ppermute | solution.py:220
  38.8 2.1 broadcast_in_dim.5
  40.8 4.3 %all-to-all-start.1 = ((bf16[4,64,2048]{2,1,0:T(8,128)(2,1)}), bf16[4,64,2048]{2,1,0:T(8,128)(2,1)}, u32[]{:S(2)}, u32[]{:S(2)}) async-start(bf16[4,64,2048]{2,1,0:T(8,128)(2,1)} %broadcast_in_dim.5), calls=%async_computation.1 | async-start | bytes 2097152 | tf_op jit(solution)/shard_map/all_to_all | solution.py:203
  45.1 12.2 %all-to-all-done.1 = bf16[4,64,2048]{2,1,0:T(8,128)(2,1)} async-done(((bf16[4,64,2048]{2,1,0:T(8,128)(2,1)}), bf16[4,64,2048]{2,1,0:T(8,128)(2,1)}, u32[]{:S(2)}, u32[]{:S(2)}) %all-to-all-start.1) | async-done | bytes 1048608 | tf_op jit(solution)/shard_map/all_to_all | solution.py:203
  57.3 26.9 %all-gather.3.cloned.1.call-done.w_ref.wo_ref = bf16[2048,1280]{1,0:T(8,128)(2,1)} async-done(((bf16[64,1280]{1,0:T(8,128)(2,1)}), bf16[2048,1280]{1,0:T(8,128)(2,1)}) %all-gather.3.cloned.1.call-update) | async-done | bytes 5242896 | tf_op jit(solution)/shard_map/all_gather | solution.py:218
  84.3 2.5 copy-done.1
  86.8 3.1 shard_map.137
  90.0 2.5 copy-done.2
  92.4 2.9 shard_map.136
  96.1 1.9 collective-permute-start.1
  98.0 15.9 %collective-permute-done.1.qb_ref = bf16[256,512]{1,0:T(8,128)(2,1)} collective-permute-done((bf16[256,512]{1,0:T(8,128)(2,1)}, bf16[256,512]{1,0:T(8,128)(2,1)}, u32[]{:S(2)}, u32[]{:S(2)}) %collective-permute-start.1) | collective-permute-done | bytes 262176 | tf_op jit(solution)/shard_map/ppermute | solution.py:239
  113.9 50.5 %all-gather.5.cloned.1.call-done.kv_ref = bf16[16384,256]{1,0:T(8,128)(2,1)} async-done(((bf16[512,256]{1,0:T(8,128)(2,1)}), bf16[16384,256]{1,0:T(8,128)(2,1)}) %all-gather.5.cloned.1.call-update) | async-done | bytes 8388624 | tf_op jit(solution)/shard_map/all_gather | solution.py:235
  164.4 65.4 %shard_map.138 = bf16[2,256,2048]{2,1,0:T(8,128)(2,1)S(1)} custom-call(s32[1]{0:T(128)} %bitcast.place_ref, bf16[256,512]{1,0:T(8,128)(2,1)S(1)} %get-tuple-element.10.qa_ref, bf16[256,512]{1,0:T(8,128)(2,1)} %collective-permute-done.1.qb_ref, bf16[16384,256]{1,0:T(8,128)(2,1)} %all-gather.5.cloned.1.call-done.kv_ref, ...), custom_call_target="tpu_custom_call" | custom-call | flops 17179869184 | bytes 16777216 | tf_op jit(solution)/shard_map/pallas_call | solution.py:144
  229.9 1.6 copy.34
  231.5 4.6 %all-to-all-start.2 = ((bf16[4,2,64,2048]{3,2,1,0:T(8,128)(2,1)}), bf16[4,2,64,2048]{3,2,1,0:T(8,128)(2,1)}, u32[]{:S(2)}, u32[]{:S(2)}) async-start(bf16[4,2,64,2048]{3,2,1,0:T(8,128)(2,1)} %bitcast.65), calls=%async_computation.2 | async-start | bytes 4194304 | tf_op jit(solution)/shard_map/all_to_all | solution.py:203
  237.0 25.2 %all-to-all-done.2 = bf16[4,2,64,2048]{3,2,1,0:T(8,128)(2,1)} async-done(((bf16[4,2,64,2048]{3,2,1,0:T(8,128)(2,1)}), bf16[4,2,64,2048]{3,2,1,0:T(8,128)(2,1)}, u32[]{:S(2)}, u32[]{:S(2)}) %all-to-all-start.2) | async-done | bytes 2097184 | tf_op jit(solution)/shard_map/all_to_all | solution.py:203
  262.2 2.1 convert_reduce_fusion
  265.3 7.9 %collective-permute-start.4 = (bf16[64,2048]{1,0:T(8,128)(2,1)S(1)}, bf16[64,2048]{1,0:T(8,128)(2,1)S(1)}, u32[]{:S(2)}, u32[]{:S(2)}) collective-permute-start(bf16[64,2048]{1,0:T(8,128)(2,1)S(1)} %get-tuple-element.8), channel_id=1, source_target_pairs={{0,252},{1,253},{2,254},{3,255},{8,244},{9,245},{10,246},{11,247},... | collective-permute-start | bytes 786440 | tf_op jit(solution)/shard_map/ppermute | solution.py:252
  273.2 1.5 collective-permute-start.2
  274.8 13.2 %collective-permute-done.2 = bf16[64,2048]{1,0:T(8,128)(2,1)S(1)} collective-permute-done((bf16[64,2048]{1,0:T(8,128)(2,1)S(1)}, bf16[64,2048]{1,0:T(8,128)(2,1)S(1)}, u32[]{:S(2)}, u32[]{:S(2)}) %collective-permute-start.2) | collective-permute-done | bytes 262176 | tf_op jit(solution)/shard_map/ppermute | solution.py:247
  288.0 1.2 fusion.24
  289.8 36.1 %all_to_all.25 = bf16[8,32,2048]{2,1,0:T(8,128)(2,1)S(1)} all-to-all(bf16[8,32,2048]{2,1,0:T(8,128)(2,1)S(1)} %bitcast.66), channel_id=1, replica_groups=mesh['ctx'=32,'exp'=8] {'exp'}, dimensions={0} | all-to-all | bytes 2097152 | tf_op jit(solution)/shard_map/all_to_all | solution.py:277
  326.9 1.9 fusion.4
  328.8 5.5 %fusion.6 = bf16[256,2048]{1,0:T(8,128)(2,1)} fusion(bf16[1,768,2048]{2,1,0:T(8,128)(2,1)S(1)} %copy-done, bf16[256,2048]{1,0:T(8,128)(2,1)} %bitcast.69, bf16[1,2048,768]{2,1,0:T(8,128)(2,1)} %param.26, f32[256,768]{1,0:T(8,128)} %fusion.4), kind=kOutput, calls=%fused_computation.7 | convolution fusion | flops 1612316672 | bytes 9175040 | tf_op jit(solution)/shard_map/dot_general | solution.py:282
  334.3 4.2 %all-to-all-start.4 = ((bf16[8,32,2048]{2,1,0:T(8,128)(2,1)}), bf16[8,32,2048]{2,1,0:T(8,128)(2,1)}, u32[]{:S(2)}, u32[]{:S(2)}) async-start(bf16[8,32,2048]{2,1,0:T(8,128)(2,1)} %bitcast.67), calls=%async_computation.4 | async-start | bytes 2097152 | tf_op jit(solution)/shard_map/all_to_all | solution.py:283
  338.6 23.1 %all-to-all-done.4 = bf16[8,32,2048]{2,1,0:T(8,128)(2,1)} async-done(((bf16[8,32,2048]{2,1,0:T(8,128)(2,1)}), bf16[8,32,2048]{2,1,0:T(8,128)(2,1)}, u32[]{:S(2)}, u32[]{:S(2)}) %all-to-all-start.4) | async-done | bytes 1048608 | tf_op jit(solution)/shard_map/all_to_all | solution.py:283
  361.7 1.6 fusion.10
  363.3 2.3 fusion.11
  (50 shorter events, 8.0 us)
Async XLA Ops:
  6.5 322.2 %copy-start = (bf16[1,768,2048]{2,1,0:T(8,128)(2,1)S(1)}, bf16[1,768,2048]{2,1,0:T(8,128)(2,1)}, u32[]{:S(2)}) copy-start(bf16[1,768,2048]{2,1,0:T(8,128)(2,1)} %param.27) | copy-start | bytes 9437188
  6.5 77.7 %all-gather.3.cloned.1.call-start = ((), (), s32[]{:S(2)}) async-start(), calls=%async_computation.5 | async-start | bytes 5406720 | tf_op jit(solution)/shard_map/all_gather | solution.py:218
  12.0 72.3 %copy-start.3 = (bf16[128]{0:T(256)(128)(2,1)S(1)}, bf16[128]{0:T(256)(128)(2,1)}, u32[]{:S(2)}) copy-start(bf16[128]{0:T(256)(128)(2,1)} %param.20) | copy-start | bytes 772
  13.1 25.7 %all-to-all-start = ((bf16[4,64,2048]{2,1,0:T(8,128)(2,1)}), bf16[4,64,2048]{2,1,0:T(8,128)(2,1)}, u32[]{:S(2)}, u32[]{:S(2)}) async-start(bf16[4,64,2048]{2,1,0:T(8,128)(2,1)} %broadcast_in_dim.4), calls=%async_computation | async-start | bytes 2097152 | tf_op jit(solution)/shard_map/all_to_all | solution.py:203
  17.4 21.4 %collective-permute-start = (bf16[64,2048]{1,0:T(8,128)(2,1)S(1)}, bf16[64,2048]{1,0:T(8,128)(2,1)}, u32[]{:S(2)}, u32[]{:S(2)}) collective-permute-start(bf16[64,2048]{1,0:T(8,128)(2,1)S(1)} %fusion.22), channel_id=1, source_target_pairs={{0,4},{1,5},{2,6},{3,7},{4,0},{5,1},{6,2},{7,3},{8,12},{9,13},{10,... | collective-permute-start | bytes 786440 | tf_op jit(solution)/shard_map/ppermute | solution.py:220
  40.8 16.5 %all-to-all-start.1 = ((bf16[4,64,2048]{2,1,0:T(8,128)(2,1)}), bf16[4,64,2048]{2,1,0:T(8,128)(2,1)}, u32[]{:S(2)}, u32[]{:S(2)}) async-start(bf16[4,64,2048]{2,1,0:T(8,128)(2,1)} %broadcast_in_dim.5), calls=%async_computation.1 | async-start | bytes 2097152 | tf_op jit(solution)/shard_map/all_to_all | solution.py:203
  45.1 119.3 %all-gather.5.cloned.1.call-start = ((), (), s32[]{:S(2)}) async-start(), calls=%async_computation.6 | async-start | bytes 8650752 | tf_op jit(solution)/shard_map/all_gather | solution.py:235
  84.3 2.5 copy-start.1
  86.8 3.2 copy-start.4
  90.0 2.5 copy-start.2
  96.1 17.8 %collective-permute-start.1 = (bf16[256,512]{1,0:T(8,128)(2,1)}, bf16[256,512]{1,0:T(8,128)(2,1)}, u32[]{:S(2)}, u32[]{:S(2)}) collective-permute-start(bf16[256,512]{1,0:T(8,128)(2,1)} %get-tuple-element.9), channel_id=1, source_target_pairs={{0,248},{8,240},{16,232},{24,224},{32,216},{40,208},{48,200},{56,1... | collective-permute-start | bytes 786440 | tf_op jit(solution)/shard_map/ppermute | solution.py:239
  231.5 4.6 %copy-start.7 = (s32[64,2]{0,1:T(2,128)S(1)}, s32[64,2]{0,1:T(2,128)}, u32[]{:S(2)}) copy-start(s32[64,2]{0,1:T(2,128)} %param.23) | copy-start | bytes 1540
  231.5 5.5 %copy-start.6 = (bf16[2048]{0:T(1024)(128)(2,1)S(1)}, bf16[2048]{0:T(1024)(128)(2,1)}, u32[]{:S(2)}) copy-start(bf16[2048]{0:T(1024)(128)(2,1)} %param.22) | copy-start | bytes 12292
  231.5 30.8 %all-to-all-start.2 = ((bf16[4,2,64,2048]{3,2,1,0:T(8,128)(2,1)}), bf16[4,2,64,2048]{3,2,1,0:T(8,128)(2,1)}, u32[]{:S(2)}, u32[]{:S(2)}) async-start(bf16[4,2,64,2048]{3,2,1,0:T(8,128)(2,1)} %bitcast.65), calls=%async_computation.2 | async-start | bytes 4194304 | tf_op jit(solution)/shard_map/all_to_all | solution.py:203
  264.4 62.5 %copy-start.9 = (bf16[1,2048,768]{2,1,0:T(8,128)(2,1)S(1)}, bf16[1,2048,768]{2,1,0:T(8,128)(2,1)}, u32[]{:S(2)}) copy-start(bf16[1,2048,768]{2,1,0:T(8,128)(2,1)} %param.25) | copy-start | bytes 9437188
  264.4 23.6 %collective-permute-start.3 = (bf16[64,2048]{1,0:T(8,128)(2,1)S(1)}, bf16[64,2048]{1,0:T(8,128)(2,1)S(1)}, u32[]{:S(2)}, u32[]{:S(2)}) collective-permute-start(bf16[64,2048]{1,0:T(8,128)(2,1)S(1)} %get-tuple-element.8), channel_id=1, source_target_pairs={{4,252},{5,253},{6,254},{7,255},{12,244},{13,245},{14,246},{15,247... | collective-permute-start | bytes 786440 | tf_op jit(solution)/shard_map/ppermute | solution.py:253
  265.3 22.8 %collective-permute-start.4 = (bf16[64,2048]{1,0:T(8,128)(2,1)S(1)}, bf16[64,2048]{1,0:T(8,128)(2,1)S(1)}, u32[]{:S(2)}, u32[]{:S(2)}) collective-permute-start(bf16[64,2048]{1,0:T(8,128)(2,1)S(1)} %get-tuple-element.8), channel_id=1, source_target_pairs={{0,252},{1,253},{2,254},{3,255},{8,244},{9,245},{10,246},{11,247},... | collective-permute-start | bytes 786440 | tf_op jit(solution)/shard_map/ppermute | solution.py:252
  273.2 14.8 %collective-permute-start.2 = (bf16[64,2048]{1,0:T(8,128)(2,1)S(1)}, bf16[64,2048]{1,0:T(8,128)(2,1)S(1)}, u32[]{:S(2)}, u32[]{:S(2)}) collective-permute-start(bf16[64,2048]{1,0:T(8,128)(2,1)S(1)} %get-tuple-element.7), channel_id=1, source_target_pairs={{4,0},{5,1},{6,2},{7,3},{12,8},{13,9},{14,10},{15,11},{20,16},{21,... | collective-permute-start | bytes 786440 | tf_op jit(solution)/shard_map/ppermute | solution.py:247
  325.9 1.0 copy-start.5
  328.8 9.8 %copy-start.8 = (s32[64,2]{0,1:T(2,128)S(1)}, s32[64,2]{0,1:T(2,128)}, u32[]{:S(2)}) copy-start(s32[64,2]{0,1:T(2,128)} %param.24) | copy-start | bytes 1540
  334.3 27.4 %all-to-all-start.4 = ((bf16[8,32,2048]{2,1,0:T(8,128)(2,1)}), bf16[8,32,2048]{2,1,0:T(8,128)(2,1)}, u32[]{:S(2)}, u32[]{:S(2)}) async-start(bf16[8,32,2048]{2,1,0:T(8,128)(2,1)} %bitcast.67), calls=%async_computation.4 | async-start | bytes 2097152 | tf_op jit(solution)/shard_map/all_to_all | solution.py:283
Sparse Core Ops, SparseCore 0:
  9.2 75.0 all-gather.2
  90.1 74.3 all-gather.4

commit v2 on v1

v2 whole, which is shorter than its diff:
```python
import functools
import math

import jax
import jax.numpy as jnp
from jax import lax
from jax.experimental import pallas as pl
from jax.experimental.pallas import tpu as pltpu
from jax.sharding import PartitionSpec as P

F32 = jnp.float32
BF16 = jnp.bfloat16
NT = (((1,), (1,)), ((), ()))
EPS = 1e-06


def normed(values, gain):
    widened = values.astype(F32)
    square = jnp.mean(widened * widened, axis=-1, keepdims=True)
    return widened * lax.rsqrt(square + EPS) * gain.astype(F32)


def params(vmem_mib):
    return pltpu.CompilerParams(vmem_limit_bytes=vmem_mib * 2**20)


def in_runs(values, ring):
    run = values.shape[0] // ring
    for job in range(2):
        yield jnp.concatenate(
            [
                values[near * run + job * run // 2 : near * run + (job + 1) * run // 2]
                for near in range(ring)
            ],
            axis=0,
        )


def kv_kernel(ring, place_ref, own_ref, other_ref, w_ref, gain_ref, out_ref):
    half, head = own_ref.shape[0], gain_ref.shape[1]
    mine = place_ref[0]
    for rows_ref, spot in ((own_ref, mine), (other_ref, 1 - mine)):
        sums = jnp.dot(rows_ref[...], w_ref[...], preferred_element_type=F32)
        for job, part in enumerate(in_runs(sums, ring)):
            keys = normed(part[:, :head], gain_ref[...]).astype(BF16)
            start = job * half + pl.multiple_of(spot * (half // 2), half // 2)
            out_ref[pl.ds(start, half // 2), :head] = keys
            for at in range(0, half // 2, head):
                block = part[at : at + head, head:].T.astype(BF16)
                out_ref[pl.ds(start + at, head), head:] = block


def q_kernel(ring, place_ref, own_ref, other_ref, w_ref, gain_ref, out_ref):
    half, head = own_ref.shape[0], gain_ref.shape[1]
    mine = place_ref[0]
    for rows_ref, spot in ((own_ref, mine), (other_ref, 1 - mine)):
        sums = jnp.dot(rows_ref[...], w_ref[...], preferred_element_type=F32)
        for job, part in enumerate(in_runs(sums, ring)):
            start = pl.multiple_of(spot * (half // 2), half // 2)
            for one in range(w_ref.shape[1] // head):
                cols = slice(one * head, (one + 1) * head)
                out_ref[job, pl.ds(start, half // 2), cols] = normed(
                    part[:, cols], gain_ref[...]
                ).astype(BF16)


def project(kernel, ring, place, own, other, weights, col_block, width, gain, out_shape):
    half, depth = own.shape
    return pl.pallas_call(
        functools.partial(kernel, ring),
        grid_spec=pltpu.PrefetchScalarGridSpec(
            num_scalar_prefetch=1,
            grid=(1,),
            in_specs=[
                pl.BlockSpec((half, depth), lambda i, p: (0, 0)),
                pl.BlockSpec((half, depth), lambda i, p: (0, 0)),
                pl.BlockSpec((depth, width), lambda i, p: (0, col_block)),
                pl.BlockSpec((1, gain.shape[0]), lambda i, p: (0, 0)),
            ],
            out_specs=pl.BlockSpec(out_shape, lambda i, p: (0,) * len(out_shape)),
        ),
        out_shape=jax.ShapeDtypeStruct(out_shape, BF16),
        compiler_params=params(40),
        cost_estimate=pl.CostEstimate(
            flops=4 * half * depth * width, bytes_accessed=8 * 2**20, transcendentals=0
        ),
    )(place, own, other, weights, gain.reshape(1, -1))


def attention_kernel(
    scale, part, place_ref, q_ref, kv_hbm, w_hbm, out_ref, kv_ref, wo_ref, qt_ref, acc_ref, att_ref, sems, wo_sem
):
    ring, jobs, sides, tile, width = out_ref.shape
    half, feats = q_ref.shape[1:]
    head = acc_ref.shape[0]
    heads = feats // head
    devices = ring * sides
    rows = devices * tile
    span = half // devices
    block = 2 * half
    chunks = sems.shape[0]
    ctx = kv_ref.shape[0] // block
    per = ctx // chunks
    place = place_ref[0]
    pair = 2
    cols = pair * rows
    longest = jnp.maximum(place, ctx - 1 - place)

    def chunk_wait(at):
        piece = pl.ds(pl.multiple_of(at * per * block, block), per * block)
        pltpu.make_async_copy(kv_hbm.at[piece], kv_ref.at[piece], sems.at[at]).wait()

    wo_copy = pltpu.make_async_copy(w_hbm.at[:, feats : 2 * feats], wo_ref, wo_sem)
    for at in range(chunks):
        @pl.when(at * per <= longest)
        def _(at=at):
            for one in range(at * per, (at + 1) * per):
                first = pl.ds(one * block, half)
                pltpu.make_async_copy(kv_hbm.at[first], kv_ref.at[first], sems.at[at]).start()
                pltpu.make_async_copy(
                    kv_hbm.at[pl.ds((ctx - 1 - one) * block + half, half)],
                    kv_ref.at[pl.ds(one * block + half, half)],
                    sems.at[at],
                ).start()

    wo_copy.start()

    for job in range(2):
        for one in range(heads):
            picked = jnp.concatenate(
                [
                    q_ref[
                        job,
                        e * span + part * tile : e * span + (part + 1) * tile,
                        one * head : (one + 1) * head,
                    ]
                    for e in range(devices)
                ],
                axis=0,
            )
            qt_ref[job, :, one * rows : (one + 1) * rows] = picked.astype(F32).T.astype(BF16)

    def one_job(turn, carry):
        own = jnp.where(turn == 0, place >= ctx - 1 - place, place < ctx - 1 - place)
        job = jnp.where(own, 0, 1)
        blocks = jnp.where(own, place, ctx - 1 - place)
        groups = heads // pair

        def steps(starts, count, state, masked=False):
            state = list(state)
            items = [(start, group) for start in starts for group in range(groups)]

            def product(item):
                start, group = item
                keys = kv_ref[pl.ds(pl.multiple_of(start, half), count), :head]
                queries = qt_ref[job, :, group * cols : (group + 1) * cols]
                return jnp.dot(keys, queries, preferred_element_type=F32)

            def collect(start, group, weights, decay):
                values = jnp.concatenate(
                    [
                        kv_ref[pl.ds(pl.multiple_of(start + i * head, head), head), head:]
                        for i in range(count // head)
                    ],
                    axis=1,
                )
                spot = slice(group * cols, (group + 1) * cols)
                acc_ref[:, spot] = acc_ref[:, spot] * decay + jnp.dot(
                    values, weights, preferred_element_type=F32
                )

            following = product(items[0])
            waiting = None
            for at, (start, group) in enumerate(items):
                scores = following
                if at + 1 < len(items):
                    following = product(items[at + 1])
                if masked:
                    key_at = lax.broadcasted_iota(jnp.int32, scores.shape, 0)
                    col = lax.broadcasted_iota(jnp.int32, scores.shape, 1) % rows
                    row_at = (col // tile * 2 + job) * span + part * tile + col % tile
                    key_at = (key_at % half // span * 2 + key_at // half) * span + key_at % span
                    scores = jnp.where(key_at <= row_at, scores, -1e30)
                before, total = state[2 * group], state[2 * group + 1]
                largest = jnp.maximum(before, jnp.max(scores, axis=0, keepdims=True))
                weights = jnp.exp2((scores - largest) * scale)
                decay = jnp.exp2((before - largest) * scale)
                state[2 * group] = largest
                state[2 * group + 1] = total * decay + jnp.sum(
                    weights.reshape(count // 8, 8, cols), axis=0
                )
                if waiting is not None:
                    collect(*waiting)
                waiting = (start, group, weights.astype(BF16), decay)
            collect(*waiting)
            return tuple(state)

        def arrive(at):
            @pl.when(turn == 0)
            def _():
                chunk_wait(at)

        def whole_chunk(at, state):
            arrive(at)
            return steps([(at * per + i) * block for i in range(per)], block, state)

        acc_ref[...] = jnp.zeros_like(acc_ref)
        state = (jnp.full((1, cols), -1e30, F32), jnp.zeros((8, cols), F32)) * groups
        full = blocks // per
        state = lax.fori_loop(0, full, whole_chunk, state)
        arrive(full)
        state = lax.fori_loop(
            full * per, blocks, lambda i, now: steps([i * block], block, now), state
        )
        state = steps([blocks * block], block, state, masked=True)
        for group in range(groups):
            total = jnp.sum(state[2 * group + 1], axis=0, keepdims=True)
            spot = slice(group * cols, (group + 1) * cols)
            acc_ref[:, spot] = acc_ref[:, spot] / total
        for one in range(heads):
            att_ref[:, one * head : (one + 1) * head] = acc_ref[
                :, one * rows : (one + 1) * rows
            ].T.astype(BF16)

        @pl.when(turn == 0)
        def _():
            wo_copy.wait()

        piece = min(512, width)
        for at in range(0, width, piece):
            sums = lax.dot_general(
                att_ref[...], wo_ref[at : at + piece, :], NT, preferred_element_type=F32
            ).astype(BF16)
            for e in range(devices):
                out_ref[e % ring, job, e // ring, :, at : at + piece] = sums[
                    e * tile : (e + 1) * tile
                ]
        return carry

    lax.fori_loop(0, 2, one_job, 0)


def attend(place, queries, kv, weights, head, ring, part, parts):
    half, feats = queries.shape[1:]
    width = weights.shape[0]
    tile = half // (2 * ring) // parts
    rows = tile * 2 * ring
    ctx = kv.shape[0] // (2 * half)
    chunks = max(1, ctx // 4)
    flops = 8 * kv.shape[0] * rows * feats
    return pl.pallas_call(
        functools.partial(attention_kernel, math.log2(math.e) / math.sqrt(head), part),
        grid_spec=pltpu.PrefetchScalarGridSpec(
            num_scalar_prefetch=1,
            grid=(1,),
            in_specs=[
                pl.BlockSpec((2, half, feats), lambda i, p: (0, 0, 0)),
                pl.BlockSpec(memory_space=pltpu.HBM),
                pl.BlockSpec(memory_space=pltpu.HBM),
            ],
            out_specs=pl.BlockSpec((ring, 2, 2, tile, width), lambda i, p: (0,) * 5),
            scratch_shapes=[
                pltpu.VMEM(kv.shape, BF16),
                pltpu.VMEM((width, feats), BF16),
                pltpu.VMEM((2, head, rows * feats // head), BF16),
                pltpu.VMEM((head, rows * feats // head), F32),
                pltpu.VMEM((rows, feats), BF16),
                pltpu.SemaphoreType.DMA((chunks,)),
                pltpu.SemaphoreType.DMA,
            ],
        ),
        out_shape=jax.ShapeDtypeStruct((ring, 2, 2, tile, width), BF16),
        compiler_params=params(58),
        cost_estimate=pl.CostEstimate(
            flops=flops, bytes_accessed=16 * 2**20, transcendentals=flops // 512
        ),
    )(place, queries, kv, weights)


def mix_kernel(tokens_ref, kept_ref, flip_ref, mirror_ref, cross_ref, gain_ref, chosen_ref, mixed_ref, sent_ref):
    half = kept_ref.shape[0]
    own = kept_ref[...] + flip_ref[...].astype(F32)
    others = mirror_ref[...].astype(F32) + cross_ref[...].astype(F32)
    mixed_ref[:half] = (tokens_ref[:half].astype(F32) + own).astype(BF16)
    mixed_ref[half:] = (tokens_ref[half:].astype(F32) + others).astype(BF16)
    rows = normed(mixed_ref[...], gain_ref[...]).astype(BF16)
    sent_ref[...] = jnp.dot(chosen_ref[...], rows, preferred_element_type=F32).astype(BF16)


def expert_kernel(rows_ref, gate_ref, up_ref, down_ref, out_ref, total_ref):
    step = pl.program_id(0)
    gate = jnp.dot(rows_ref[...], gate_ref[...], preferred_element_type=F32)
    up = jnp.dot(rows_ref[...], up_ref[...], preferred_element_type=F32)
    hidden = (gate / (1.0 + jnp.exp(-gate)) * up).astype(BF16)
    share = jnp.dot(hidden, down_ref[...], preferred_element_type=F32)

    @pl.when(step == 0)
    def _():
        total_ref[...] = share

    @pl.when(step > 0)
    def _():
        total_ref[...] += share

    @pl.when(step == pl.num_programs(0) - 1)
    def _():
        out_ref[...] = total_ref[...].astype(BF16)


def run_experts(rows, gate_weight, up_weight, down_weight):
    count, width = rows.shape
    inner = gate_weight.shape[1]
    piece = math.gcd(inner, 256)
    return pl.pallas_call(
        expert_kernel,
        grid=(inner // piece,),
        in_specs=[
            pl.BlockSpec((count, width), lambda i: (0, 0)),
            pl.BlockSpec((width, piece), lambda i: (0, i)),
            pl.BlockSpec((width, piece), lambda i: (0, i)),
            pl.BlockSpec((piece, width), lambda i: (i, 0)),
        ],
        out_specs=pl.BlockSpec((count, width), lambda i: (0, 0)),
        scratch_shapes=[pltpu.VMEM((count, width), F32)],
        out_shape=jax.ShapeDtypeStruct((count, width), BF16),
        compiler_params=params(40),
        cost_estimate=pl.CostEstimate(
            flops=6 * count * width * inner,
            bytes_accessed=6 * width * inner,
            transcendentals=count * inner,
        ),
    )(rows, gate_weight, up_weight, down_weight)


def shards(
    tokens,
    attn_gain,
    q_weight,
    k_weight,
    v_weight,
    q_gain,
    k_gain,
    out_weight,
    moe_gain,
    expert_ids,
    route_code,
    gate_weight,
    up_weight,
    expert_down_matrix,
):
    exp_count = lax.axis_size("exp")
    ctx_count = lax.axis_size("ctx")
    ctx_place = lax.axis_index("ctx")
    exp_place = lax.axis_index("exp")
    tok_rows, width = tokens.shape
    head = q_gain.shape[0]
    feats = q_weight.shape[1]
    group_size = feats * exp_count // k_weight.shape[1]
    kv_first = exp_place * (feats // head) // group_size * head
    ring = exp_count // 2
    half_rows = tok_rows * ring
    far = exp_place // ring
    near = exp_place % ring
    rings = [list(range(ring)), list(range(ring, exp_count))]
    flip = [(e, (e + ring) % exp_count) for e in range(exp_count)]
    mirror = [(c, ctx_count - 1 - c) for c in range(ctx_count)]

    def over_ring(parts):
        return lax.all_to_all(parts, "exp", 0, 0, tiled=True, axis_index_groups=rings)

    def to_ring(rows):
        spread = jnp.broadcast_to(rows[None], (ring,) + rows.shape)
        return over_ring(spread).reshape(half_rows, width)

    packed = jnp.concatenate(
        [
            q_weight,
            out_weight.T,
            lax.dynamic_slice_in_dim(k_weight, kv_first, head, 1),
            lax.dynamic_slice_in_dim(v_weight, kv_first, head, 1),
        ],
        axis=1,
    )
    weights = lax.all_gather(packed, "ctx", axis=0, tiled=True)
    normal_rows = normed(tokens, attn_gain).astype(BF16)
    half_tile = tok_rows // 2
    mirrored = lax.ppermute(normal_rows[half_tile:], "ctx", mirror)
    worked = jnp.concatenate([normal_rows[:half_tile], mirrored], axis=0)
    flipped = lax.ppermute(worked, "exp", flip)
    own = to_ring(worked)
    flipped, own = lax.optimization_barrier((flipped, own))
    other = to_ring(flipped)
    far_index = far.astype(jnp.int32).reshape(1)
    kv = project(
        kv_kernel,
        ring,
        far_index,
        own,
        other,
        weights,
        feats // head,
        2 * head,
        k_gain,
        (2 * half_rows, 2 * head),
    )
    kv_all = lax.all_gather(kv, "ctx", axis=0, tiled=True)
    queries = project(
        q_kernel, ring, far_index, own, other, weights, 0, feats, q_gain, (2, half_rows, feats)
    )
    cross = [
        (c * exp_count + e, (ctx_count - 1 - c) * exp_count + (e + ring) % exp_count)
        for c in range(ctx_count)
        for e in range(exp_count)
    ]
    ctx_index = ctx_place.astype(jnp.int32).reshape(1)
    shares = []
    for part in range(2):
        sums = attend(ctx_index, queries, kv_all, weights, head, ring, part, 2)
        if part == 0:
            raw, ids, sums = lax.optimization_barrier((tokens, expert_ids, sums))
            partner = lax.ppermute(raw, "exp", flip)
            partner_ids = lax.ppermute(ids, "exp", flip)
        shares.append(jnp.sum(over_ring(sums).astype(F32), axis=0))
    shares = jnp.concatenate(shares, axis=2)
    rounded = shares.astype(BF16).reshape(2, tok_rows, width)
    by_flip = lax.ppermute(rounded[0], "exp", flip)
    by_mirror = lax.ppermute(rounded[1], "ctx", mirror)
    by_cross = lax.ppermute(rounded[1], ("ctx", "exp"), cross)

    def by_side(mine, theirs):
        return jnp.where(far == 0, jnp.stack([mine, theirs]), jnp.stack([theirs, mine]))

    sides = by_side(tokens, partner).reshape(2, 2, half_tile, width)
    sides = sides.swapaxes(0, 1).reshape(2 * tok_rows, width)
    top_count = expert_ids.shape[1]
    capacity = min(tok_rows, 2 * tok_rows * top_count // exp_count)
    places = jnp.arange(exp_count * capacity, dtype=jnp.int32)

    def slots_of(ids, experts):
        flat = ids.reshape(-1)
        one_hot = (flat[:, None] == experts[None, :]).astype(jnp.int32)
        earlier = jnp.cumsum(one_hot, axis=0) - one_hot
        rank = jnp.sum(earlier * one_hot, axis=1)
        known = jnp.sum(one_hot, axis=1) > 0
        slots = jnp.where(known, (flat - experts[0]) * capacity + rank, -1)
        return slots.reshape(tok_rows, top_count)

    near_experts = jnp.arange(ring, dtype=jnp.int32) + far * ring
    both_slots = jnp.stack(
        [slots_of(side, near_experts) for side in by_side(expert_ids, partner_ids)]
    )
    expert_of, rank_of = both_slots // capacity, both_slots % capacity
    side_of = jnp.arange(2, dtype=jnp.int32)[:, None, None]
    rows_of = jnp.where(both_slots < 0, -1, (expert_of * 2 + side_of) * capacity + rank_of)
    rows_of = rows_of.reshape(2, 2, half_tile, top_count).swapaxes(0, 1)
    rows_of = rows_of.reshape(2 * tok_rows, top_count)
    chosen = jnp.any(places[:, None, None] == rows_of[None], axis=-1).astype(BF16)
    mixed_both, sent = pl.pallas_call(
        mix_kernel,
        out_shape=(
            jax.ShapeDtypeStruct(sides.shape, BF16),
            jax.ShapeDtypeStruct((exp_count * capacity, width), BF16),
        ),
        compiler_params=params(40),
    )(
        sides,
        shares[0].reshape(tok_rows, width),
        by_flip,
        by_mirror,
        by_cross,
        moe_gain.reshape(1, -1),
        chosen,
    )
    mixed_both = mixed_both.reshape(2, 2, half_tile, width)
    mixed = lax.dynamic_index_in_dim(mixed_both, far, 1, keepdims=False).reshape(tok_rows, width)
    arrived = over_ring(sent.reshape(ring, 2 * capacity, width)).reshape(-1, width)
    done = run_experts(arrived, gate_weight[0], up_weight[0], expert_down_matrix[0])
    done = done.reshape(ring, 2, capacity, width).swapaxes(0, 1)
    back = lax.all_to_all(
        done.reshape(exp_count, capacity, width), "exp", split_axis=0, concat_axis=0, tiled=True
    ).reshape(exp_count * capacity, width)
    slots = slots_of(expert_ids, jnp.arange(exp_count, dtype=jnp.int32))
    codes = route_code.astype(F32)
    route_weight = codes / jnp.sum(codes, axis=-1, keepdims=True)
    total = mixed.astype(F32)
    for j in range(top_count):
        pick = (slots[:, j : j + 1] == places[None, :]).astype(BF16)
        picked = jnp.dot(pick, back, preferred_element_type=F32)
        total = total + picked * route_weight[:, j : j + 1]
    return total.astype(BF16)


def solution(mesh):
    placed = (
        P(("ctx", "exp"), None),
        P(),
        P("ctx", "exp"),
        P("ctx", None),
        P("ctx", None),
        P(),
        P(),
        P("exp", "ctx"),
        P(),
        P(("ctx", "exp"), None),
        P(("ctx", "exp"), None),
        P("exp", None, None),
        P("exp", None, None),
        P("exp", None, None),
    )
    return jax.shard_map(
        shards, mesh=mesh, in_specs=placed, out_specs=P(("ctx", "exp"), None), check_vma=False
    )
```

time: 373 us -> 329 us (0.88)
  the two profiles are of different devices: /device:TPU:65 before, /device:TPU:8 now
where the time goes in v2:
time: 329 us; the launch traced here: 326 us
  waiting for transfers between devices  178 us (54%)
  Pallas kernels  50.4 us (15%)
  starting transfers between devices  46.2 us (14%)
  blocking collectives  17.5 us (5%)
  between operations  13.8 us (4%)
  local copies, waits for them, and re-layouts  13 us (4%)
  other arithmetic  6.28 us (2%)
    all_gather x1, waiting for transfers between devices, shards(): kv_all = lax.all_gather(kv, 'ctx', axis=0, tiled=True)  64.2 us
    pallas_call x2, Pallas kernels, attend(): pl.pallas_call(functools.partial(attention_kernel, math.log2(math.e) / ma...  42.1 us
    all_to_all x1, waiting for transfers between devices, shards(): lax.all_to_all(done.reshape(exp_count, capacity, width), 'exp', split_axi...  26.5 us
    all_to_all x4, waiting for transfers between devices, over_ring(): lax.all_to_all(parts, 'exp', 0, 0, tiled=True, axis_index_groups=rings)  25.5 us
    all_gather x1, waiting for transfers between devices, shards(): weights = lax.all_gather(packed, 'ctx', axis=0, tiled=True)  24.2 us
    ppermute x1, waiting for transfers between devices, shards(): by_flip = lax.ppermute(rounded[0], 'exp', flip)  22 us
    all_to_all x1, blocking collectives, over_ring(): lax.all_to_all(parts, 'exp', 0, 0, tiled=True, axis_index_groups=rings)  17.5 us
    all_to_all x4, starting transfers between devices, over_ring(): lax.all_to_all(parts, 'exp', 0, 0, tiled=True, axis_index_groups=rings)  16.9 us
  transfers between devices with their start and end apart: 14, of which 8 were waited for; matrix products, arithmetic and copies ran while one was open for 3% of the time, Pallas kernels for 7%

profile of v2, /device:TPU:8, one launch (start us, length us, event | category | flops | bytes accessed | tf_op | source)
XLA Modules:
  0.0 326.1 jit_solution(2802607005441345495)
XLA Ops:
  8.1 1.6 pad_maximum_fusion.2
  10.4 1.1 fusion.4
  11.5 1.1 fusion.6
  12.6 5.2 %collective-permute-start = (bf16[32,2048]{1,0:T(8,128)(2,1)S(1)}, bf16[32,2048]{1,0:T(8,128)(2,1)S(1)}, u32[]{:S(2)}, u32[]{:S(2)}) collective-permute-start(bf16[32,2048]{1,0:T(8,128)(2,1)S(1)} %get-tuple-element.30), channel_id=1, source_target_pairs={{0,248},{8,240},{16,232},{24,224},{32,216},{40,208},{48,200},{56,1... | collective-permute-start | bytes 393224 | tf_op jit(solution)/shard_map/ppermute | solution.py:387
  17.8 3.9 %collective-permute-done = bf16[32,2048]{1,0:T(8,128)(2,1)S(1)} collective-permute-done((bf16[32,2048]{1,0:T(8,128)(2,1)S(1)}, bf16[32,2048]{1,0:T(8,128)(2,1)S(1)}, u32[]{:S(2)}, u32[]{:S(2)}) %collective-permute-start) | collective-permute-done | bytes 131104 | tf_op jit(solution)/shard_map/ppermute | solution.py:387
  21.7 1.1 broadcast_in_dim.15
  22.8 4.3 %all-to-all-start = ((bf16[4,64,2048]{2,1,0:T(8,128)(2,1)}), bf16[4,64,2048]{2,1,0:T(8,128)(2,1)S(1)}, u32[]{:S(2)}, u32[]{:S(2)}) async-start(bf16[4,64,2048]{2,1,0:T(8,128)(2,1)} %broadcast_in_dim.15), calls=%async_computation | async-start | bytes 2097152 | tf_op jit(solution)/shard_map/all_to_all | solution.py:369
  27.1 6.8 %collective-permute-start.1 = (bf16[64,2048]{1,0:T(8,128)(2,1)S(1)}, bf16[64,2048]{1,0:T(8,128)(2,1)S(1)}, u32[]{:S(2)}, u32[]{:S(2)}) collective-permute-start(bf16[64,2048]{1,0:T(8,128)(2,1)S(1)} %pad_maximum_fusion.1), channel_id=1, source_target_pairs={{0,4},{1,5},{2,6},{3,7},{4,0},{5,1},{6,2},{7,3},{8,12},{9,13},{10,... | collective-permute-start | bytes 786440 | tf_op jit(solution)/shard_map/ppermute | solution.py:389
  33.9 11.2 %collective-permute-done.1 = bf16[64,2048]{1,0:T(8,128)(2,1)S(1)} collective-permute-done((bf16[64,2048]{1,0:T(8,128)(2,1)S(1)}, bf16[64,2048]{1,0:T(8,128)(2,1)S(1)}, u32[]{:S(2)}, u32[]{:S(2)}) %collective-permute-start.1) | collective-permute-done | bytes 262176 | tf_op jit(solution)/shard_map/ppermute | solution.py:389
  45.1 1.1 broadcast_in_dim.17
  46.2 3.5 %all-to-all-start.1 = ((bf16[4,64,2048]{2,1,0:T(8,128)(2,1)}), bf16[4,64,2048]{2,1,0:T(8,128)(2,1)S(1)}, u32[]{:S(2)}, u32[]{:S(2)}) async-start(bf16[4,64,2048]{2,1,0:T(8,128)(2,1)} %broadcast_in_dim.17), calls=%async_computation.1 | async-start | bytes 2097152 | tf_op jit(solution)/shard_map/all_to_all | solution.py:369
  49.8 11.8 %all-to-all-done.1 = bf16[4,64,2048]{2,1,0:T(8,128)(2,1)S(1)} async-done(((bf16[4,64,2048]{2,1,0:T(8,128)(2,1)}), bf16[4,64,2048]{2,1,0:T(8,128)(2,1)S(1)}, u32[]{:S(2)}, u32[]{:S(2)}) %all-to-all-start.1) | async-done | bytes 1048608 | tf_op jit(solution)/shard_map/all_to_all | solution.py:369
  61.5 24.2 %all-gather.3.cloned.1.call-done.w_ref.w_hbm = bf16[2048,1280]{1,0:T(8,128)(2,1)} async-done(((bf16[64,1280]{1,0:T(8,128)(2,1)}), bf16[2048,1280]{1,0:T(8,128)(2,1)}) %all-gather.3.cloned.1.call-update) | async-done | bytes 5242896 | tf_op jit(solution)/shard_map/all_gather | solution.py:384
  85.7 2.5 copy-done.1
  88.2 1.6 shard_map.137
  90.6 2.5 copy-done.2
  93.1 1.5 shard_map.136.q_ref
  95.4 64.2 %all-gather.5.cloned.1.call-done.kv_hbm = bf16[16384,256]{1,0:T(8,128)(2,1)} async-done(((bf16[512,256]{1,0:T(8,128)(2,1)}), bf16[16384,256]{1,0:T(8,128)(2,1)}) %all-gather.5.cloned.1.call-update) | async-done | bytes 8388624 | tf_op jit(solution)/shard_map/all_gather | solution.py:406
  159.6 21.1 %shard_map.138 = bf16[4,2,2,16,2048]{4,3,2,1,0:T(8,128)(2,1)} custom-call(s32[1]{0:T(128)} %bitcast.2.place_ref, bf16[2,256,512]{2,1,0:T(8,128)(2,1)} %copy-done.6, bf16[16384,256]{1,0:T(8,128)(2,1)} %all-gather.5.cloned.1.call-done.kv_hbm, bf16[2048,1280]{1,0:T(8,128)(2,1)} %all-gather.3.cloned.1.call-done.w_ref.w_hbm), custom_call_target="tpu_custom_call" | custom-call | flops 8589934592 | bytes 16777216 | tf_op jit(solution)/shard_map/pallas_call | solution.py:251
  180.7 4.3 %all-to-all-start.2 = ((bf16[4,2,2,16,2048]{4,3,2,1,0:T(8,128)(2,1)}), bf16[4,2,2,16,2048]{4,3,2,1,0:T(8,128)(2,1)S(1)}, u32[]{:S(2)}, u32[]{:S(2)}) async-start(bf16[4,2,2,16,2048]{4,3,2,1,0:T(8,128)(2,1)} %shard_map.138), calls=%async_computation.2 | async-start | bytes 2097152 | tf_op jit(solution)/shard_map/all_to_all | solution.py:369
  184.9 3.2 collective-permute-start.6
  188.2 2.7 collective-permute-start.2
  190.9 21.0 %shard_map.139 = bf16[4,2,2,16,2048]{4,3,2,1,0:T(8,128)(2,1)} custom-call(s32[1]{0:T(128)} %bitcast.2.place_ref, bf16[2,256,512]{2,1,0:T(8,128)(2,1)} %copy-done.6, bf16[16384,256]{1,0:T(8,128)(2,1)} %all-gather.5.cloned.1.call-done.kv_hbm, bf16[2048,1280]{1,0:T(8,128)(2,1)} %all-gather.3.cloned.1.call-done.w_ref.w_hbm), custom_call_target="tpu_custom_call" | custom-call | flops 8589934592 | bytes 16777216 | tf_op jit(solution)/shard_map/pallas_call | solution.py:251
  214.1 4.8 %all-to-all-start.3 = ((bf16[4,2,2,16,2048]{4,3,2,1,0:T(8,128)(2,1)}), bf16[4,2,2,16,2048]{4,3,2,1,0:T(8,128)(2,1)S(1)}, u32[]{:S(2)}, u32[]{:S(2)}) async-start(bf16[4,2,2,16,2048]{4,3,2,1,0:T(8,128)(2,1)} %shard_map.139), calls=%async_computation.3 | async-start | bytes 2097152 | tf_op jit(solution)/shard_map/all_to_all | solution.py:369
  219.5 13.8 %all-to-all-done.3 = bf16[4,2,2,16,2048]{4,3,2,1,0:T(8,128)(2,1)S(1)} async-done(((bf16[4,2,2,16,2048]{4,3,2,1,0:T(8,128)(2,1)}), bf16[4,2,2,16,2048]{4,3,2,1,0:T(8,128)(2,1)S(1)}, u32[]{:S(2)}, u32[]{:S(2)}) %all-to-all-start.3) | async-done | bytes 1048608 | tf_op jit(solution)/shard_map/all_to_all | solution.py:369
  233.6 4.4 %collective-permute-start.4 = (bf16[64,2048]{1,0:T(8,128)(2,1)S(1)}, bf16[64,2048]{1,0:T(8,128)(2,1)S(1)}, u32[]{:S(2)}, u32[]{:S(2)}) collective-permute-start(bf16[64,2048]{1,0:T(8,128)(2,1)S(1)} %bitcast.79), channel_id=1, source_target_pairs={{0,248},{8,240},{16,232},{24,224},{32,216},{40,208},{48,200},{56,1... | collective-permute-start | bytes 786440 | tf_op jit(solution)/shard_map/ppermute | solution.py:427
  238.0 2.7 collective-permute-start.3
  240.8 22.0 %collective-permute-done.3.flip_ref = bf16[64,2048]{1,0:T(8,128)(2,1)S(1)} collective-permute-done((bf16[64,2048]{1,0:T(8,128)(2,1)S(1)}, bf16[64,2048]{1,0:T(8,128)(2,1)S(1)}, u32[]{:S(2)}, u32[]{:S(2)}) %collective-permute-start.3) | collective-permute-done | bytes 262176 | tf_op jit(solution)/shard_map/ppermute | solution.py:426
  263.6 17.5 %all_to_all.30 = bf16[4,64,2048]{2,1,0:T(8,128)(2,1)S(1)} all-to-all(bf16[4,64,2048]{2,1,0:T(8,128)(2,1)S(1)} %bitcast.69), channel_id=1, replica_groups={{0,1,2,3},{4,5,6,7},{8,9,10,11},{12,13,14,15},{16,17,18,19},{20,21,22,2..., dimensions={0} | all-to-all | bytes 2097152 | tf_op jit(solution)/shard_map/all_to_all | solution.py:369
  281.1 4.4 %shard_map.141 = bf16[256,2048]{1,0:T(8,128)(2,1)S(1)} custom-call(bf16[256,2048]{1,0:T(8,128)(2,1)S(1)} %bitcast.62, bf16[2048,768]{1,0:T(8,128)(2,1)S(1)} %bitcast.64, bf16[2048,768]{1,0:T(8,128)(2,1)S(1)} %bitcast.65, bf16[768,2048]{1,0:T(8,128)(2,1)S(1)} %bitcast.66), custom_call_target="tpu_custom_call" | custom-call | flops 2415919104 | bytes 9437184 | tf_op jit(solution)/shard_map/pallas_call | solution.py:314
  286.6 4.2 %all-to-all-start.5 = ((bf16[8,32,2048]{2,1,0:T(8,128)(2,1)}), bf16[8,32,2048]{2,1,0:T(8,128)(2,1)S(1)}, u32[]{:S(2)}, u32[]{:S(2)}) async-start(bf16[8,32,2048]{2,1,0:T(8,128)(2,1)} %bitcast.33), calls=%async_computation.5 | async-start | bytes 2097152 | tf_op jit(solution)/shard_map/all_to_all | solution.py:479
  291.4 26.5 %all-to-all-done.5 = bf16[8,32,2048]{2,1,0:T(8,128)(2,1)S(1)} async-done(((bf16[8,32,2048]{2,1,0:T(8,128)(2,1)}), bf16[8,32,2048]{2,1,0:T(8,128)(2,1)S(1)}, u32[]{:S(2)}, u32[]{:S(2)}) %all-to-all-start.5) | async-done | bytes 1048608 | tf_op jit(solution)/shard_map/all_to_all | solution.py:479
  (99 shorter events, 10.8 us)
Async XLA Ops:
  6.5 0.8 copy-start
  6.5 79.2 %all-gather.3.cloned.1.call-start = ((), (), s32[]{:S(2)}) async-start(), calls=%async_computation.6 | async-start | bytes 5406720 | tf_op jit(solution)/shard_map/all_gather | solution.py:384
  12.6 9.1 %collective-permute-start = (bf16[32,2048]{1,0:T(8,128)(2,1)S(1)}, bf16[32,2048]{1,0:T(8,128)(2,1)S(1)}, u32[]{:S(2)}, u32[]{:S(2)}) collective-permute-start(bf16[32,2048]{1,0:T(8,128)(2,1)S(1)} %get-tuple-element.30), channel_id=1, source_target_pairs={{0,248},{8,240},{16,232},{24,224},{32,216},{40,208},{48,200},{56,1... | collective-permute-start | bytes 393224 | tf_op jit(solution)/shard_map/ppermute | solution.py:387
  21.7 64.0 %copy-start.7 = (bf16[128]{0:T(256)(128)(2,1)S(1)}, bf16[128]{0:T(256)(128)(2,1)}, u32[]{:S(2)}) copy-start(bf16[128]{0:T(256)(128)(2,1)} %param.20) | copy-start | bytes 772
  22.8 22.3 %all-to-all-start = ((bf16[4,64,2048]{2,1,0:T(8,128)(2,1)}), bf16[4,64,2048]{2,1,0:T(8,128)(2,1)S(1)}, u32[]{:S(2)}, u32[]{:S(2)}) async-start(bf16[4,64,2048]{2,1,0:T(8,128)(2,1)} %broadcast_in_dim.15), calls=%async_computation | async-start | bytes 2097152 | tf_op jit(solution)/shard_map/all_to_all | solution.py:369
  27.1 18.0 %collective-permute-start.1 = (bf16[64,2048]{1,0:T(8,128)(2,1)S(1)}, bf16[64,2048]{1,0:T(8,128)(2,1)S(1)}, u32[]{:S(2)}, u32[]{:S(2)}) collective-permute-start(bf16[64,2048]{1,0:T(8,128)(2,1)S(1)} %pad_maximum_fusion.1), channel_id=1, source_target_pairs={{0,4},{1,5},{2,6},{3,7},{4,0},{5,1},{6,2},{7,3},{8,12},{9,13},{10,... | collective-permute-start | bytes 786440 | tf_op jit(solution)/shard_map/ppermute | solution.py:389
  46.2 15.3 %all-to-all-start.1 = ((bf16[4,64,2048]{2,1,0:T(8,128)(2,1)}), bf16[4,64,2048]{2,1,0:T(8,128)(2,1)S(1)}, u32[]{:S(2)}, u32[]{:S(2)}) async-start(bf16[4,64,2048]{2,1,0:T(8,128)(2,1)} %broadcast_in_dim.17), calls=%async_computation.1 | async-start | bytes 2097152 | tf_op jit(solution)/shard_map/all_to_all | solution.py:369
  49.7 109.9 %all-gather.5.cloned.1.call-start = ((), (), s32[]{:S(2)}) async-start(), calls=%async_computation.7 | async-start | bytes 8650752 | tf_op jit(solution)/shard_map/all_gather | solution.py:406
  85.7 2.5 copy-start.1
  88.2 1.7 copy-start.11
  88.2 1.7 copy-start.10
  88.2 2.4 copy-start.8
  90.6 2.5 copy-start.2
  94.6 0.8 copy-start.6
  159.6 28.6 %copy-start.9 = (bf16[64,2048]{1,0:T(8,128)(2,1)S(1)}, bf16[64,2048]{1,0:T(8,128)(2,1)}, u32[]{:S(2)}) copy-start(bf16[64,2048]{1,0:T(8,128)(2,1)} %param.14) | copy-start | bytes 786436
  180.7 33.4 %all-to-all-start.2 = ((bf16[4,2,2,16,2048]{4,3,2,1,0:T(8,128)(2,1)}), bf16[4,2,2,16,2048]{4,3,2,1,0:T(8,128)(2,1)S(1)}, u32[]{:S(2)}, u32[]{:S(2)}) async-start(bf16[4,2,2,16,2048]{4,3,2,1,0:T(8,128)(2,1)} %shard_map.138), calls=%async_computation.2 | async-start | bytes 2097152 | tf_op jit(solution)/shard_map/all_to_all | solution.py:369
  184.9 27.0 %collective-permute-start.6 = (s32[64,2]{0,1:T(2,128)S(1)}, s32[64,2]{0,1:T(2,128)S(1)}, u32[]{:S(2)}, u32[]{:S(2)}) collective-permute-start(s32[64,2]{0,1:T(2,128)S(1)} %copy-done.10), channel_id=1, source_target_pairs={{0,4},{1,5},{2,6},{3,7},{4,0},{5,1},{6,2},{7,3},{8,12},{9,13},{10,... | collective-permute-start | bytes 1544 | tf_op jit(solution)/shard_map/ppermute | solution.py:422
  188.2 52.6 %collective-permute-start.2 = (bf16[64,2048]{1,0:T(8,128)(2,1)S(1)}, bf16[64,2048]{1,0:T(8,128)(2,1)S(1)}, u32[]{:S(2)}, u32[]{:S(2)}) collective-permute-start(bf16[64,2048]{1,0:T(8,128)(2,1)S(1)} %copy-done.9), channel_id=1, source_target_pairs={{0,4},{1,5},{2,6},{3,7},{4,0},{5,1},{6,2},{7,3},{8,12},{9,13},{10,... | collective-permute-start | bytes 786440 | tf_op jit(solution)/shard_map/ppermute | solution.py:421
  214.1 19.2 %all-to-all-start.3 = ((bf16[4,2,2,16,2048]{4,3,2,1,0:T(8,128)(2,1)}), bf16[4,2,2,16,2048]{4,3,2,1,0:T(8,128)(2,1)S(1)}, u32[]{:S(2)}, u32[]{:S(2)}) async-start(bf16[4,2,2,16,2048]{4,3,2,1,0:T(8,128)(2,1)} %shard_map.139), calls=%async_computation.3 | async-start | bytes 2097152 | tf_op jit(solution)/shard_map/all_to_all | solution.py:369
  233.2 47.9 %copy-start.5 = (bf16[1,768,2048]{2,1,0:T(8,128)(2,1)S(1)}, bf16[1,768,2048]{2,1,0:T(8,128)(2,1)}, u32[]{:S(2)}) copy-start(bf16[1,768,2048]{2,1,0:T(8,128)(2,1)} %param.27) | copy-start | bytes 9437188
  233.5 29.3 %collective-permute-start.5 = (bf16[64,2048]{1,0:T(8,128)(2,1)S(1)}, bf16[64,2048]{1,0:T(8,128)(2,1)S(1)}, u32[]{:S(2)}, u32[]{:S(2)}) collective-permute-start(bf16[64,2048]{1,0:T(8,128)(2,1)S(1)} %bitcast.78), channel_id=1, source_target_pairs={{0,252},{1,253},{2,254},{3,255},{4,248},{5,249},{6,250},{7,251},{8... | collective-permute-start | bytes 786440 | tf_op jit(solution)/shard_map/ppermute | solution.py:428
  233.6 29.2 %collective-permute-start.4 = (bf16[64,2048]{1,0:T(8,128)(2,1)S(1)}, bf16[64,2048]{1,0:T(8,128)(2,1)S(1)}, u32[]{:S(2)}, u32[]{:S(2)}) collective-permute-start(bf16[64,2048]{1,0:T(8,128)(2,1)S(1)} %bitcast.79), channel_id=1, source_target_pairs={{0,248},{8,240},{16,232},{24,224},{32,216},{40,208},{48,200},{56,1... | collective-permute-start | bytes 786440 | tf_op jit(solution)/shard_map/ppermute | solution.py:427
  238.0 24.8 %collective-permute-start.3 = (bf16[64,2048]{1,0:T(8,128)(2,1)S(1)}, bf16[64,2048]{1,0:T(8,128)(2,1)S(1)}, u32[]{:S(2)}, u32[]{:S(2)}) collective-permute-start(bf16[64,2048]{1,0:T(8,128)(2,1)S(1)} %bitcast.80), channel_id=1, source_target_pairs={{0,4},{1,5},{2,6},{3,7},{4,0},{5,1},{6,2},{7,3},{8,12},{9,13},{10,... | collective-permute-start | bytes 786440 | tf_op jit(solution)/shard_map/ppermute | solution.py:426
  240.7 40.4 %copy-start.3 = (bf16[1,2048,768]{2,1,0:T(8,128)(2,1)S(1)}, bf16[1,2048,768]{2,1,0:T(8,128)(2,1)}, u32[]{:S(2)}) copy-start(bf16[1,2048,768]{2,1,0:T(8,128)(2,1)} %param.25) | copy-start | bytes 9437188
  240.7 40.4 %copy-start.4 = (bf16[1,2048,768]{2,1,0:T(8,128)(2,1)S(1)}, bf16[1,2048,768]{2,1,0:T(8,128)(2,1)}, u32[]{:S(2)}) copy-start(bf16[1,2048,768]{2,1,0:T(8,128)(2,1)} %param.26) | copy-start | bytes 9437188
  285.5 5.5 %copy-start.12 = (s32[64,2]{0,1:T(2,128)S(1)}, s32[64,2]{0,1:T(2,128)}, u32[]{:S(2)}) copy-start(s32[64,2]{0,1:T(2,128)} %param.24) | copy-start | bytes 1540
  286.6 31.3 %all-to-all-start.5 = ((bf16[8,32,2048]{2,1,0:T(8,128)(2,1)}), bf16[8,32,2048]{2,1,0:T(8,128)(2,1)S(1)}, u32[]{:S(2)}, u32[]{:S(2)}) async-start(bf16[8,32,2048]{2,1,0:T(8,128)(2,1)} %bitcast.33), calls=%async_computation.5 | async-start | bytes 2097152 | tf_op jit(solution)/shard_map/all_to_all | solution.py:479
Sparse Core Ops, SparseCore 0:
  9.8 75.9 all-gather.2
  90.0 69.5 all-gather.4

commit v3 on v2

--- a/solution.py
+++ b/solution.py
@@ -80,7 +80,7 @@
             out_specs=pl.BlockSpec(out_shape, lambda i, p: (0,) * len(out_shape)),
         ),
         out_shape=jax.ShapeDtypeStruct(out_shape, BF16),
-        compiler_params=params(40),
+        compiler_params=params(58),
         cost_estimate=pl.CostEstimate(
             flops=4 * half * depth * width, bytes_accessed=8 * 2**20, transcendentals=0
         ),
@@ -102,7 +102,7 @@
     ctx = kv_ref.shape[0] // block
     per = ctx // chunks
     place = place_ref[0]
-    pair = 2
+    pair = 4
     cols = pair * rows
     longest = jnp.maximum(place, ctx - 1 - place)
 
@@ -146,7 +146,8 @@
         blocks = jnp.where(own, place, ctx - 1 - place)
         groups = heads // pair
 
-        def steps(starts, count, state, masked=False):
+        def steps(starts, state, masked=False):
+            count = block
             state = list(state)
             items = [(start, group) for start in starts for group in range(groups)]
 
@@ -175,7 +176,7 @@
                 scores = following
                 if at + 1 < len(items):
                     following = product(items[at + 1])
-                if masked:
+                if masked and at // groups == len(starts) - 1:
                     key_at = lax.broadcasted_iota(jnp.int32, scores.shape, 0)
                     col = lax.broadcasted_iota(jnp.int32, scores.shape, 1) % rows
                     row_at = (col // tile * 2 + job) * span + part * tile + col % tile
@@ -202,17 +203,20 @@
 
         def whole_chunk(at, state):
             arrive(at)
-            return steps([(at * per + i) * block for i in range(per)], block, state)
+            return steps([(at * per + i) * block for i in range(per)], state)
 
         acc_ref[...] = jnp.zeros_like(acc_ref)
         state = (jnp.full((1, cols), -1e30, F32), jnp.zeros((8, cols), F32)) * groups
         full = blocks // per
         state = lax.fori_loop(0, full, whole_chunk, state)
         arrive(full)
-        state = lax.fori_loop(
-            full * per, blocks, lambda i, now: steps([i * block], block, now), state
-        )
-        state = steps([blocks * block], block, state, masked=True)
+        tails = [
+            lambda now, left=left: steps(
+                [(blocks - left + i) * block for i in range(left + 1)], now, masked=True
+            )
+            for left in range(per)
+        ]
+        state = lax.switch(blocks - full * per, tails, state)
         for group in range(groups):
             total = jnp.sum(state[2 * group + 1], axis=0, keepdims=True)
             spot = slice(group * cols, (group + 1) * cols)
@@ -277,12 +281,20 @@
     )(place, queries, kv, weights)
 
 
-def mix_kernel(tokens_ref, kept_ref, flip_ref, mirror_ref, cross_ref, gain_ref, chosen_ref, mixed_ref, sent_ref):
-    half = kept_ref.shape[0]
-    own = kept_ref[...] + flip_ref[...].astype(F32)
-    others = mirror_ref[...].astype(F32) + cross_ref[...].astype(F32)
-    mixed_ref[:half] = (tokens_ref[:half].astype(F32) + own).astype(BF16)
-    mixed_ref[half:] = (tokens_ref[half:].astype(F32) + others).astype(BF16)
+def mix_kernel(*refs):
+    *part_refs, gain_ref, chosen_ref, mixed_ref, sent_ref = refs
+    parts = len(part_refs) // 4
+    for part in range(parts):
+        kept_ref, flip_ref, mirror_ref, cross_ref = part_refs[4 * part : 4 * part + 4]
+        sides, tile, width = kept_ref.shape
+        sums = (
+            kept_ref[...] + flip_ref[...].astype(F32),
+            mirror_ref[...].astype(F32) + cross_ref[...].astype(F32),
+        )
+        for job in range(2):
+            for side in range(sides):
+                start = ((job * sides + side) * parts + part) * tile
+                mixed_ref[start : start + tile] = sums[job][side].astype(BF16)
     rows = normed(mixed_ref[...], gain_ref[...]).astype(BF16)
     sent_ref[...] = jnp.dot(chosen_ref[...], rows, preferred_element_type=F32).astype(BF16)
 
@@ -323,13 +335,34 @@
         out_specs=pl.BlockSpec((count, width), lambda i: (0, 0)),
         scratch_shapes=[pltpu.VMEM((count, width), F32)],
         out_shape=jax.ShapeDtypeStruct((count, width), BF16),
-        compiler_params=params(40),
+        compiler_params=params(58),
         cost_estimate=pl.CostEstimate(
             flops=6 * count * width * inner,
             bytes_accessed=6 * width * inner,
             transcendentals=count * inner,
         ),
     )(rows, gate_weight, up_weight, down_weight)
+
+
+def combine_kernel(back_ref, rows_ref, weight_ref, base_ref, out_ref):
+    total = base_ref[...].astype(F32)
+    places = lax.broadcasted_iota(jnp.int32, (rows_ref.shape[0], back_ref.shape[0]), 1)
+    for j in range(rows_ref.shape[1]):
+        pick = (rows_ref[:, j : j + 1] == places).astype(F32).astype(BF16)
+        picked = jnp.dot(pick, back_ref[...], preferred_element_type=F32)
+        total = total + picked * weight_ref[:, j : j + 1]
+    out_ref[...] = total.astype(out_ref.dtype)
+
+
+def combine(back, rows, weight, base, dtype):
+    return pl.pallas_call(
+        combine_kernel,
+        out_shape=jax.ShapeDtypeStruct(base.shape, dtype),
+        compiler_params=params(40),
+        cost_estimate=pl.CostEstimate(
+            flops=4 * rows.shape[0] * back.size, bytes_accessed=2 * back.size, transcendentals=0
+        ),
+    )(back, rows, weight, base)
 
 
 def shards(
@@ -382,10 +415,12 @@
         axis=1,
     )
     weights = lax.all_gather(packed, "ctx", axis=0, tiled=True)
-    normal_rows = normed(tokens, attn_gain).astype(BF16)
     half_tile = tok_rows // 2
-    mirrored = lax.ppermute(normal_rows[half_tile:], "ctx", mirror)
-    worked = jnp.concatenate([normal_rows[:half_tile], mirrored], axis=0)
+    mirrored = lax.ppermute(tokens[half_tile:], "ctx", mirror)
+    raw = jnp.concatenate([tokens[:half_tile], mirrored], axis=0)
+    worked = normed(raw, attn_gain).astype(BF16)
+    routes = jnp.concatenate([expert_ids, route_code], axis=1)
+    partner_routes = lax.ppermute(routes, "exp", flip)
     flipped = lax.ppermute(worked, "exp", flip)
     own = to_ring(worked)
     flipped, own = lax.optimization_barrier((flipped, own))
@@ -413,25 +448,27 @@
         for e in range(exp_count)
     ]
     ctx_index = ctx_place.astype(jnp.int32).reshape(1)
-    shares = []
+    mine = (jnp.arange(2) == far)[None, :, None, None]
+    residual = raw.reshape(2, 1, 2, half_tile // 2, width)
+    mixed_parts = []
+    rounded = None
     for part in range(2):
         sums = attend(ctx_index, queries, kv_all, weights, head, ring, part, 2)
-        if part == 0:
-            raw, ids, sums = lax.optimization_barrier((tokens, expert_ids, sums))
-            partner = lax.ppermute(raw, "exp", flip)
-            partner_ids = lax.ppermute(ids, "exp", flip)
-        shares.append(jnp.sum(over_ring(sums).astype(F32), axis=0))
-    shares = jnp.concatenate(shares, axis=2)
-    rounded = shares.astype(BF16).reshape(2, tok_rows, width)
-    by_flip = lax.ppermute(rounded[0], "exp", flip)
-    by_mirror = lax.ppermute(rounded[1], "ctx", mirror)
-    by_cross = lax.ppermute(rounded[1], ("ctx", "exp"), cross)
+        if part:
+            sums, rounded = lax.optimization_barrier((sums, rounded))
+        shares = jnp.sum(over_ring(sums).astype(F32), axis=0)
+        shares = shares + jnp.where(mine, residual[:, :, part].astype(F32), 0.0)
+        rounded = shares.astype(BF16)
+        mixed_parts += [
+            shares[0],
+            lax.ppermute(rounded[0], "exp", flip),
+            lax.ppermute(rounded[1], "ctx", mirror),
+            lax.ppermute(rounded[1], ("ctx", "exp"), cross),
+        ]
 
     def by_side(mine, theirs):
         return jnp.where(far == 0, jnp.stack([mine, theirs]), jnp.stack([theirs, mine]))
 
-    sides = by_side(tokens, partner).reshape(2, 2, half_tile, width)
-    sides = sides.swapaxes(0, 1).reshape(2 * tok_rows, width)
     top_count = expert_ids.shape[1]
     capacity = min(tok_rows, 2 * tok_rows * top_count // exp_count)
     places = jnp.arange(exp_count * capacity, dtype=jnp.int32)
@@ -446,48 +483,37 @@
         return slots.reshape(tok_rows, top_count)
 
     near_experts = jnp.arange(ring, dtype=jnp.int32) + far * ring
-    both_slots = jnp.stack(
-        [slots_of(side, near_experts) for side in by_side(expert_ids, partner_ids)]
-    )
+    both_routes = by_side(routes, partner_routes)
+    both_slots = jnp.stack([slots_of(side[:, :top_count], near_experts) for side in both_routes])
     expert_of, rank_of = both_slots // capacity, both_slots % capacity
     side_of = jnp.arange(2, dtype=jnp.int32)[:, None, None]
     rows_of = jnp.where(both_slots < 0, -1, (expert_of * 2 + side_of) * capacity + rank_of)
-    rows_of = rows_of.reshape(2, 2, half_tile, top_count).swapaxes(0, 1)
-    rows_of = rows_of.reshape(2 * tok_rows, top_count)
-    chosen = jnp.any(places[:, None, None] == rows_of[None], axis=-1).astype(BF16)
+    sorted_rows = rows_of.reshape(2, 2, half_tile, top_count).swapaxes(0, 1)
+    sorted_rows = sorted_rows.reshape(2 * tok_rows, top_count)
+    chosen = jnp.any(places[:, None, None] == sorted_rows[None], axis=-1).astype(BF16)
+    codes = both_routes[:, :, top_count:].astype(F32)
+    route_weight = codes / jnp.sum(codes, axis=-1, keepdims=True)
     mixed_both, sent = pl.pallas_call(
         mix_kernel,
         out_shape=(
-            jax.ShapeDtypeStruct(sides.shape, BF16),
+            jax.ShapeDtypeStruct((2 * tok_rows, width), BF16),
             jax.ShapeDtypeStruct((exp_count * capacity, width), BF16),
         ),
         compiler_params=params(40),
-    )(
-        sides,
-        shares[0].reshape(tok_rows, width),
-        by_flip,
-        by_mirror,
-        by_cross,
-        moe_gain.reshape(1, -1),
-        chosen,
-    )
+    )(*mixed_parts, moe_gain.reshape(1, -1), chosen)
     mixed_both = mixed_both.reshape(2, 2, half_tile, width)
     mixed = lax.dynamic_index_in_dim(mixed_both, far, 1, keepdims=False).reshape(tok_rows, width)
     arrived = over_ring(sent.reshape(ring, 2 * capacity, width)).reshape(-1, width)
     done = run_experts(arrived, gate_weight[0], up_weight[0], expert_down_matrix[0])
-    done = done.reshape(ring, 2, capacity, width).swapaxes(0, 1)
-    back = lax.all_to_all(
-        done.reshape(exp_count, capacity, width), "exp", split_axis=0, concat_axis=0, tiled=True
-    ).reshape(exp_count * capacity, width)
-    slots = slots_of(expert_ids, jnp.arange(exp_count, dtype=jnp.int32))
-    codes = route_code.astype(F32)
-    route_weight = codes / jnp.sum(codes, axis=-1, keepdims=True)
-    total = mixed.astype(F32)
-    for j in range(top_count):
-        pick = (slots[:, j : j + 1] == places[None, :]).astype(BF16)
-        picked = jnp.dot(pick, back, preferred_element_type=F32)
-        total = total + picked * route_weight[:, j : j + 1]
-    return total.astype(BF16)
+    back = over_ring(done.reshape(ring, 2 * capacity, width)).reshape(-1, width)
+    theirs, mine = (
+        [lax.dynamic_index_in_dim(a, side, 0, keepdims=False) for a in (rows_of, route_weight)]
+        for side in (1 - far, far)
+    )
+    given = combine(back, *theirs, jnp.zeros((tok_rows, width), F32), BF16)
+    returned = lax.ppermute(given, "exp", flip)
+    total = combine(back, *mine, mixed, F32)
+    return (total + returned.astype(F32)).astype(BF16)
 
 
 def solution(mesh):

time: 329 us -> 308 us (0.936)
  waiting for transfers between devices: 178 us -> 156 us
  starting transfers between devices: 46.2 us -> 53.7 us
  local copies, waits for them, and re-layouts: 13 us -> 5.87 us
  Pallas kernels: 50.4 us -> 54.6 us
    all_to_all x1 -> x0, waiting for transfers between devices: 26.5 us -> none  [shards(): lax.all_to_all(done.reshape(exp_count, capacity, width), 'exp', split_axi...]
    all_gather x1, waiting for transfers between devices: 64.2 us -> 53.8 us  [shards(): kv_all = lax.all_gather(kv, 'ctx', axis=0, tiled=True)]
    ppermute x6 -> x9, starting transfers between devices: 18.3 us -> 25.6 us  [the longest x2 8.07 us: shards(): lax.ppermute(rounded[1], ('ctx', 'exp'), cross)]
    all_to_all x4 -> x5, waiting for transfers between devices: 25.5 us -> 32.4 us  [over_ring(): lax.all_to_all(parts, 'exp', 0, 0, tiled=True, axis_index_groups=rings)]
    unnamed x28 -> x11, local copies, waits for them, and re-layouts: 6.72 us -> 0.02 us
    pallas_call x2, Pallas kernels: 42.1 us -> 36.7 us  [attend(): pl.pallas_call(functools.partial(attention_kernel, math.log2(math.e) / ma...]
    pallas_call x2, Pallas kernels: 3.09 us -> 8.12 us  [project(): pl.pallas_call(functools.partial(kernel, ring), grid_spec=pltpu.PrefetchS...]
    ppermute x6 -> x9, waiting for transfers between devices: 25.9 us -> 30.8 us  [the longest x1 12.9 us: shards(): returned = lax.ppermute(given, 'exp', flip)]
  transfers between devices with their start and end apart: 14 -> 17, of which waited for: 8 -> 10; matrix products, arithmetic and copies ran while one was open for 3% -> 3% of each run, Pallas kernels for 7% -> 8%
where the time goes in v3:
time: 308 us; the launch traced here: 307 us
  waiting for transfers between devices  156 us (51%)
  Pallas kernels  54.6 us (18%)
  starting transfers between devices  53.7 us (17%)
  blocking collectives  18.5 us (6%)
  between operations  13.8 us (4%)
  local copies, waits for them, and re-layouts  5.87 us (2%)
  other arithmetic  5.22 us (2%)
    all_gather x1, waiting for transfers between devices, shards(): kv_all = lax.all_gather(kv, 'ctx', axis=0, tiled=True)  53.8 us
    pallas_call x2, Pallas kernels, attend(): pl.pallas_call(functools.partial(attention_kernel, math.log2(math.e) / ma...  36.7 us
    all_to_all x5, waiting for transfers between devices, over_ring(): lax.all_to_all(parts, 'exp', 0, 0, tiled=True, axis_index_groups=rings)  32.4 us
    all_gather x1, waiting for transfers between devices, shards(): weights = lax.all_gather(packed, 'ctx', axis=0, tiled=True)  27.4 us
    all_to_all x5, starting transfers between devices, over_ring(): lax.all_to_all(parts, 'exp', 0, 0, tiled=True, axis_index_groups=rings)  21.4 us
    all_to_all x1, blocking collectives, over_ring(): lax.all_to_all(parts, 'exp', 0, 0, tiled=True, axis_index_groups=rings)  18.5 us
    ppermute x1, waiting for transfers between devices, shards(): returned = lax.ppermute(given, 'exp', flip)  12.9 us
    ppermute x1, waiting for transfers between devices, shards(): flipped = lax.ppermute(worked, 'exp', flip)  11.2 us
  transfers between devices with their start and end apart: 17, of which 10 were waited for; matrix products, arithmetic and copies ran while one was open for 3% of the time, Pallas kernels for 8%

profile of v3, /device:TPU:8, one launch (start us, length us, event | category | flops | bytes accessed | tf_op | source)
XLA Modules:
  0.0 307.2 jit_solution(13700357869585020486)
XLA Ops:
  7.3 1.6 pad_maximum_fusion.1
  9.8 5.2 %collective-permute-start = (bf16[32,2048]{1,0:T(8,128)(2,1)S(1)}, bf16[32,2048]{1,0:T(8,128)(2,1)S(1)}, u32[]{:S(2)}, u32[]{:S(2)}) collective-permute-start(bf16[32,2048]{1,0:T(8,128)(2,1)S(1)} %get-tuple-element.32), channel_id=1, source_target_pairs={{0,248},{8,240},{16,232},{24,224},{32,216},{40,208},{48,200},{56,1... | collective-permute-start | bytes 393224 | tf_op jit(solution)/shard_map/ppermute | solution.py:419
  15.7 3.2 %collective-permute-done = bf16[32,2048]{1,0:T(8,128)(2,1)S(1)} collective-permute-done((bf16[32,2048]{1,0:T(8,128)(2,1)S(1)}, bf16[32,2048]{1,0:T(8,128)(2,1)S(1)}, u32[]{:S(2)}, u32[]{:S(2)}) %collective-permute-start) | collective-permute-done | bytes 131104 | tf_op jit(solution)/shard_map/ppermute | solution.py:419
  20.4 4.3 %all-to-all-start = ((bf16[4,64,2048]{2,1,0:T(8,128)(2,1)}), bf16[4,64,2048]{2,1,0:T(8,128)(2,1)S(1)}, u32[]{:S(2)}, u32[]{:S(2)}) async-start(bf16[4,64,2048]{2,1,0:T(8,128)(2,1)} %broadcast_in_dim.63), calls=%async_computation | async-start | bytes 2097152 | tf_op jit(solution)/shard_map/all_to_all | solution.py:402
  24.6 6.8 %collective-permute-start.1 = (bf16[64,2048]{1,0:T(8,128)(2,1)S(1)}, bf16[64,2048]{1,0:T(8,128)(2,1)S(1)}, u32[]{:S(2)}, u32[]{:S(2)}) collective-permute-start(bf16[64,2048]{1,0:T(8,128)(2,1)S(1)} %fusion.2), channel_id=1, source_target_pairs={{0,4},{1,5},{2,6},{3,7},{4,0},{5,1},{6,2},{7,3},{8,12},{9,13},{10,... | collective-permute-start | bytes 786440 | tf_op jit(solution)/shard_map/ppermute | solution.py:424
  31.4 11.2 %collective-permute-done.1 = bf16[64,2048]{1,0:T(8,128)(2,1)S(1)} collective-permute-done((bf16[64,2048]{1,0:T(8,128)(2,1)S(1)}, bf16[64,2048]{1,0:T(8,128)(2,1)S(1)}, u32[]{:S(2)}, u32[]{:S(2)}) %collective-permute-start.1) | collective-permute-done | bytes 262176 | tf_op jit(solution)/shard_map/ppermute | solution.py:424
  42.6 1.2 broadcast_in_dim.64
  43.8 4.5 %all-to-all-start.1 = ((bf16[4,64,2048]{2,1,0:T(8,128)(2,1)}), bf16[4,64,2048]{2,1,0:T(8,128)(2,1)S(1)}, u32[]{:S(2)}, u32[]{:S(2)}) async-start(bf16[4,64,2048]{2,1,0:T(8,128)(2,1)} %broadcast_in_dim.64), calls=%async_computation.1 | async-start | bytes 2097152 | tf_op jit(solution)/shard_map/all_to_all | solution.py:402
  48.3 10.9 %all-to-all-done.1 = bf16[4,64,2048]{2,1,0:T(8,128)(2,1)S(1)} async-done(((bf16[4,64,2048]{2,1,0:T(8,128)(2,1)}), bf16[4,64,2048]{2,1,0:T(8,128)(2,1)S(1)}, u32[]{:S(2)}, u32[]{:S(2)}) %all-to-all-start.1) | async-done | bytes 1048608 | tf_op jit(solution)/shard_map/all_to_all | solution.py:402
  59.2 27.4 %all-gather.3.cloned.1.call-done.w_ref.w_hbm = bf16[2048,1280]{1,0:T(8,128)(2,1)} async-done(((bf16[64,1280]{1,0:T(8,128)(2,1)}), bf16[2048,1280]{1,0:T(8,128)(2,1)}) %all-gather.3.cloned.1.call-update) | async-done | bytes 5242896 | tf_op jit(solution)/shard_map/all_gather | solution.py:417
  86.6 3.5 %shard_map.137 = bf16[512,256]{1,0:T(8,128)(2,1)} custom-call(s32[1]{0:T(128)} %bitcast.1.place_ref, bf16[256,2048]{1,0:T(8,128)(2,1)} %bitcast.79, bf16[256,2048]{1,0:T(8,128)(2,1)} %bitcast.81, bf16[2048,1280]{1,0:T(8,128)(2,1)} %all-gather.3.cloned.1.call-done.w_ref.w_hbm, bf16[1,128]{1,0:T(2,128)(2,1)} %bitcast.97), custom_call_target="tpu_custom_call" | custom-call | flops 536870912 | bytes 8388608 | tf_op jit(solution)/shard_map/pallas_call | solution.py:69
  90.2 4.0 %collective-permute-start.8 = (s32[64,4]{0,1:T(4,128)S(1)}, s32[64,4]{0,1:T(4,128)S(1)}, u32[]{:S(2)}, u32[]{:S(2)}) collective-permute-start(s32[64,4]{0,1:T(4,128)S(1)} %get-tuple-element.42), channel_id=1, source_target_pairs={{0,4},{1,5},{2,6},{3,7},{4,0},{5,1},{6,2},{7,3},{8,12},{9,13},{10,... | collective-permute-start | bytes 3080 | tf_op jit(solution)/shard_map/ppermute | solution.py:423
  94.2 3.6 %collective-permute-done.8 = s32[64,4]{0,1:T(4,128)S(1)} collective-permute-done((s32[64,4]{0,1:T(4,128)S(1)}, s32[64,4]{0,1:T(4,128)S(1)}, u32[]{:S(2)}, u32[]{:S(2)}) %collective-permute-start.8) | collective-permute-done | bytes 1056 | tf_op jit(solution)/shard_map/ppermute | solution.py:423
  100.3 4.6 %shard_map.136.q_ref = bf16[2,256,512]{2,1,0:T(8,128)(2,1)} custom-call(s32[1]{0:T(128)} %bitcast.1.place_ref, bf16[256,2048]{1,0:T(8,128)(2,1)} %bitcast.80, bf16[256,2048]{1,0:T(8,128)(2,1)} %bitcast.82, bf16[2048,1280]{1,0:T(8,128)(2,1)} %all-gather.3.cloned.1.call-done.w_ref.w_hbm, bf16[1,128]{1,0:T(2,128)(2,1)} %bitcast.98), custom_call_target="tpu_custom_call" | custom-call | flops 1073741824 | bytes 8388608 | tf_op jit(solution)/shard_map/pallas_call | solution.py:69
  104.9 53.8 %all-gather.5.cloned.1.call-done.kv_hbm = bf16[16384,256]{1,0:T(8,128)(2,1)} async-done(((bf16[512,256]{1,0:T(8,128)(2,1)}), bf16[16384,256]{1,0:T(8,128)(2,1)}) %all-gather.5.cloned.1.call-update) | async-done | bytes 8388624 | tf_op jit(solution)/shard_map/all_gather | solution.py:441
  158.7 18.3 %shard_map.138 = bf16[4,2,2,16,2048]{4,3,2,1,0:T(8,128)(2,1)} custom-call(s32[1]{0:T(128)} %bitcast.place_ref, bf16[2,256,512]{2,1,0:T(8,128)(2,1)} %shard_map.136.q_ref, bf16[16384,256]{1,0:T(8,128)(2,1)} %all-gather.5.cloned.1.call-done.kv_hbm, bf16[2048,1280]{1,0:T(8,128)(2,1)} %all-gather.3.cloned.1.call-done.w_ref.w_hbm), custom_call_target="tpu_custom_call" | custom-call | flops 8589934592 | bytes 16777216 | tf_op jit(solution)/shard_map/pallas_call | solution.py:255
  177.1 4.2 %all-to-all-start.2 = ((bf16[4,2,2,16,2048]{4,3,2,1,0:T(8,128)(2,1)}), bf16[4,2,2,16,2048]{4,3,2,1,0:T(8,128)(2,1)S(1)}, u32[]{:S(2)}, u32[]{:S(2)}) async-start(bf16[4,2,2,16,2048]{4,3,2,1,0:T(8,128)(2,1)} %shard_map.138), calls=%async_computation.2 | async-start | bytes 2097152 | tf_op jit(solution)/shard_map/all_to_all | solution.py:402
  181.3 18.4 %shard_map.139 = bf16[4,2,2,16,2048]{4,3,2,1,0:T(8,128)(2,1)} custom-call(s32[1]{0:T(128)} %bitcast.place_ref, bf16[2,256,512]{2,1,0:T(8,128)(2,1)} %shard_map.136.q_ref, bf16[16384,256]{1,0:T(8,128)(2,1)} %all-gather.5.cloned.1.call-done.kv_hbm, bf16[2048,1280]{1,0:T(8,128)(2,1)} %all-gather.3.cloned.1.call-done.w_ref.w_hbm), custom_call_target="tpu_custom_call" | custom-call | flops 8589934592 | bytes 16777216 | tf_op jit(solution)/shard_map/pallas_call | solution.py:255
  200.0 4.8 %all-to-all-start.3 = ((bf16[4,2,2,16,2048]{4,3,2,1,0:T(8,128)(2,1)}), bf16[4,2,2,16,2048]{4,3,2,1,0:T(8,128)(2,1)S(1)}, u32[]{:S(2)}, u32[]{:S(2)}) async-start(bf16[4,2,2,16,2048]{4,3,2,1,0:T(8,128)(2,1)} %shard_map.139), calls=%async_computation.3 | async-start | bytes 2097152 | tf_op jit(solution)/shard_map/all_to_all | solution.py:402
  204.8 1.2 collective-permute-start.3
  206.0 3.5 %collective-permute-start.4 = (bf16[2,16,2048]{2,1,0:T(8,128)(2,1)S(1)}, bf16[2,16,2048]{2,1,0:T(8,128)(2,1)S(1)}, u32[]{:S(2)}, u32[]{:S(2)}) collective-permute-start(bf16[2,16,2048]{2,1,0:T(8,128)(2,1)S(1)} %get-tuple-element.29), channel_id=1, source_target_pairs={{0,252},{1,253},{2,254},{3,255},{4,248},{5,249},{6,250},{7,251},{8... | collective-permute-start | bytes 393224 | tf_op jit(solution)/shard_map/ppermute | solution.py:466
  209.5 2.5 collective-permute-start.2
  212.1 7.9 %all-to-all-done.3 = bf16[4,2,2,16,2048]{4,3,2,1,0:T(8,128)(2,1)S(1)} async-done(((bf16[4,2,2,16,2048]{4,3,2,1,0:T(8,128)(2,1)}), bf16[4,2,2,16,2048]{4,3,2,1,0:T(8,128)(2,1)S(1)}, u32[]{:S(2)}, u32[]{:S(2)}) %all-to-all-start.3) | async-done | bytes 1048608 | tf_op jit(solution)/shard_map/all_to_all | solution.py:402
  220.4 4.6 %collective-permute-start.7 = (bf16[2,16,2048]{2,1,0:T(8,128)(2,1)S(1)}, bf16[2,16,2048]{2,1,0:T(8,128)(2,1)S(1)}, u32[]{:S(2)}, u32[]{:S(2)}) collective-permute-start(bf16[2,16,2048]{2,1,0:T(8,128)(2,1)S(1)} %get-tuple-element.25), channel_id=1, source_target_pairs={{0,252},{1,253},{2,254},{3,255},{4,248},{5,249},{6,250},{7,251},{8... | collective-permute-start | bytes 393224 | tf_op jit(solution)/shard_map/ppermute | solution.py:466
  225.0 2.5 collective-permute-start.5
  227.6 11.0 %collective-permute-done.5.refs_5_ = bf16[2,16,2048]{2,1,0:T(8,128)(2,1)S(1)} collective-permute-done((bf16[2,16,2048]{2,1,0:T(8,128)(2,1)S(1)}, bf16[2,16,2048]{2,1,0:T(8,128)(2,1)S(1)}, u32[]{:S(2)}, u32[]{:S(2)}) %collective-permute-start.5) | collective-permute-done | bytes 131104 | tf_op jit(solution)/shard_map/ppermute | solution.py:464
  239.3 18.5 %all_to_all.30 = bf16[4,64,2048]{2,1,0:T(8,128)(2,1)} all-to-all(bf16[4,64,2048]{2,1,0:T(8,128)(2,1)S(1)} %bitcast.76), channel_id=1, replica_groups={{0,1,2,3},{4,5,6,7},{8,9,10,11},{12,13,14,15},{16,17,18,19},{20,21,22,2..., dimensions={0} | all-to-all | bytes 2097152 | tf_op jit(solution)/shard_map/all_to_all | solution.py:402
  257.8 8.0 %shard_map.141 = bf16[256,2048]{1,0:T(8,128)(2,1)} custom-call(bf16[256,2048]{1,0:T(8,128)(2,1)} %bitcast.84, bf16[2048,768]{1,0:T(8,128)(2,1)} %bitcast.85, bf16[2048,768]{1,0:T(8,128)(2,1)} %bitcast.86, bf16[768,2048]{1,0:T(8,128)(2,1)} %bitcast.87), custom_call_target="tpu_custom_call" | custom-call | flops 2415919104 | bytes 9437184 | tf_op jit(solution)/shard_map/pallas_call | solution.py:326
  265.8 3.5 %all-to-all-start.5 = ((bf16[4,64,2048]{2,1,0:T(8,128)(2,1)}), bf16[4,64,2048]{2,1,0:T(8,128)(2,1)S(1)}, u32[]{:S(2)}, u32[]{:S(2)}) async-start(bf16[4,64,2048]{2,1,0:T(8,128)(2,1)} %bitcast.83), calls=%async_computation.5 | async-start | bytes 2097152 | tf_op jit(solution)/shard_map/all_to_all | solution.py:402
  269.9 13.6 %all-to-all-done.5 = bf16[4,64,2048]{2,1,0:T(8,128)(2,1)S(1)} async-done(((bf16[4,64,2048]{2,1,0:T(8,128)(2,1)}), bf16[4,64,2048]{2,1,0:T(8,128)(2,1)S(1)}, u32[]{:S(2)}, u32[]{:S(2)}) %all-to-all-start.5) | async-done | bytes 1048608 | tf_op jit(solution)/shard_map/all_to_all | solution.py:402
  284.0 2.0 collective-permute-start.9
  286.7 12.9 %collective-permute-done.9 = bf16[64,2048]{1,0:T(8,128)(2,1)S(1)} collective-permute-done((bf16[64,2048]{1,0:T(8,128)(2,1)S(1)}, bf16[64,2048]{1,0:T(8,128)(2,1)S(1)}, u32[]{:S(2)}, u32[]{:S(2)}) %collective-permute-start.9) | collective-permute-done | bytes 262176 | tf_op jit(solution)/shard_map/ppermute | solution.py:514
  (84 shorter events, 10.2 us)
Async XLA Ops:
  6.5 80.1 %all-gather.3.cloned.1.call-start = ((), (), s32[]{:S(2)}) async-start(), calls=%async_computation.6 | async-start | bytes 5406720 | tf_op jit(solution)/shard_map/all_gather | solution.py:417
  9.8 9.1 %collective-permute-start = (bf16[32,2048]{1,0:T(8,128)(2,1)S(1)}, bf16[32,2048]{1,0:T(8,128)(2,1)S(1)}, u32[]{:S(2)}, u32[]{:S(2)}) collective-permute-start(bf16[32,2048]{1,0:T(8,128)(2,1)S(1)} %get-tuple-element.32), channel_id=1, source_target_pairs={{0,248},{8,240},{16,232},{24,224},{32,216},{40,208},{48,200},{56,1... | collective-permute-start | bytes 393224 | tf_op jit(solution)/shard_map/ppermute | solution.py:419
  20.4 22.3 %all-to-all-start = ((bf16[4,64,2048]{2,1,0:T(8,128)(2,1)}), bf16[4,64,2048]{2,1,0:T(8,128)(2,1)S(1)}, u32[]{:S(2)}, u32[]{:S(2)}) async-start(bf16[4,64,2048]{2,1,0:T(8,128)(2,1)} %broadcast_in_dim.63), calls=%async_computation | async-start | bytes 2097152 | tf_op jit(solution)/shard_map/all_to_all | solution.py:402
  24.6 18.0 %collective-permute-start.1 = (bf16[64,2048]{1,0:T(8,128)(2,1)S(1)}, bf16[64,2048]{1,0:T(8,128)(2,1)S(1)}, u32[]{:S(2)}, u32[]{:S(2)}) collective-permute-start(bf16[64,2048]{1,0:T(8,128)(2,1)S(1)} %fusion.2), channel_id=1, source_target_pairs={{0,4},{1,5},{2,6},{3,7},{4,0},{5,1},{6,2},{7,3},{8,12},{9,13},{10,... | collective-permute-start | bytes 786440 | tf_op jit(solution)/shard_map/ppermute | solution.py:424
  42.6 44.0 %copy-start = (bf16[4,64,2048]{2,1,0:T(8,128)(2,1)}, bf16[4,64,2048]{2,1,0:T(8,128)(2,1)S(1)}, u32[]{:S(2)}) copy-start(bf16[4,64,2048]{2,1,0:T(8,128)(2,1)S(1)} %all-to-all-done) | copy-start | bytes 3145732
  43.8 15.4 %all-to-all-start.1 = ((bf16[4,64,2048]{2,1,0:T(8,128)(2,1)}), bf16[4,64,2048]{2,1,0:T(8,128)(2,1)S(1)}, u32[]{:S(2)}, u32[]{:S(2)}) async-start(bf16[4,64,2048]{2,1,0:T(8,128)(2,1)} %broadcast_in_dim.64), calls=%async_computation.1 | async-start | bytes 2097152 | tf_op jit(solution)/shard_map/all_to_all | solution.py:402
  48.3 110.4 %all-gather.5.cloned.1.call-start = ((), (), s32[]{:S(2)}) async-start(), calls=%async_computation.7 | async-start | bytes 8650752 | tf_op jit(solution)/shard_map/all_gather | solution.py:441
  59.2 27.4 %copy-start.1 = (bf16[4,64,2048]{2,1,0:T(8,128)(2,1)}, bf16[4,64,2048]{2,1,0:T(8,128)(2,1)S(1)}, u32[]{:S(2)}) copy-start(bf16[4,64,2048]{2,1,0:T(8,128)(2,1)S(1)} %all-to-all-done.1) | copy-start | bytes 3145732
  86.6 3.5 %copy-start.3 = (s32[64,2]{0,1:T(2,128)S(1)}, s32[64,2]{0,1:T(2,128)}, u32[]{:S(2)}) copy-start(s32[64,2]{0,1:T(2,128)} %param.24) | copy-start | bytes 1540
  86.6 3.5 %copy-start.4 = (s32[64,2]{0,1:T(2,128)S(1)}, s32[64,2]{0,1:T(2,128)}, u32[]{:S(2)}) copy-start(s32[64,2]{0,1:T(2,128)} %param.23) | copy-start | bytes 1540
  86.6 7.6 %copy-start.2 = (bf16[2048]{0:T(1024)(128)(2,1)S(1)}, bf16[2048]{0:T(1024)(128)(2,1)}, u32[]{:S(2)}) copy-start(bf16[2048]{0:T(1024)(128)(2,1)} %param.22) | copy-start | bytes 12292
  90.2 7.6 %collective-permute-start.8 = (s32[64,4]{0,1:T(4,128)S(1)}, s32[64,4]{0,1:T(4,128)S(1)}, u32[]{:S(2)}, u32[]{:S(2)}) collective-permute-start(s32[64,4]{0,1:T(4,128)S(1)} %get-tuple-element.42), channel_id=1, source_target_pairs={{0,4},{1,5},{2,6},{3,7},{4,0},{5,1},{6,2},{7,3},{8,12},{9,13},{10,... | collective-permute-start | bytes 3080 | tf_op jit(solution)/shard_map/ppermute | solution.py:423
  177.1 22.6 %all-to-all-start.2 = ((bf16[4,2,2,16,2048]{4,3,2,1,0:T(8,128)(2,1)}), bf16[4,2,2,16,2048]{4,3,2,1,0:T(8,128)(2,1)S(1)}, u32[]{:S(2)}, u32[]{:S(2)}) async-start(bf16[4,2,2,16,2048]{4,3,2,1,0:T(8,128)(2,1)} %shard_map.138), calls=%async_computation.2 | async-start | bytes 2097152 | tf_op jit(solution)/shard_map/all_to_all | solution.py:402
  200.0 20.0 %all-to-all-start.3 = ((bf16[4,2,2,16,2048]{4,3,2,1,0:T(8,128)(2,1)}), bf16[4,2,2,16,2048]{4,3,2,1,0:T(8,128)(2,1)S(1)}, u32[]{:S(2)}, u32[]{:S(2)}) async-start(bf16[4,2,2,16,2048]{4,3,2,1,0:T(8,128)(2,1)} %shard_map.139), calls=%async_computation.3 | async-start | bytes 2097152 | tf_op jit(solution)/shard_map/all_to_all | solution.py:402
  204.8 22.7 %collective-permute-start.3 = (bf16[2,16,2048]{2,1,0:T(8,128)(2,1)S(1)}, bf16[2,16,2048]{2,1,0:T(8,128)(2,1)S(1)}, u32[]{:S(2)}, u32[]{:S(2)}) collective-permute-start(bf16[2,16,2048]{2,1,0:T(8,128)(2,1)S(1)} %get-tuple-element.29), channel_id=1, source_target_pairs={{0,248},{8,240},{16,232},{24,224},{32,216},{40,208},{48,200},{56,1... | collective-permute-start | bytes 393224 | tf_op jit(solution)/shard_map/ppermute | solution.py:465
  206.0 21.5 %collective-permute-start.4 = (bf16[2,16,2048]{2,1,0:T(8,128)(2,1)S(1)}, bf16[2,16,2048]{2,1,0:T(8,128)(2,1)S(1)}, u32[]{:S(2)}, u32[]{:S(2)}) collective-permute-start(bf16[2,16,2048]{2,1,0:T(8,128)(2,1)S(1)} %get-tuple-element.29), channel_id=1, source_target_pairs={{0,252},{1,253},{2,254},{3,255},{4,248},{5,249},{6,250},{7,251},{8... | collective-permute-start | bytes 393224 | tf_op jit(solution)/shard_map/ppermute | solution.py:466
  209.5 15.5 %collective-permute-start.2 = (bf16[2,16,2048]{2,1,0:T(8,128)(2,1)S(1)}, bf16[2,16,2048]{2,1,0:T(8,128)(2,1)S(1)}, u32[]{:S(2)}, u32[]{:S(2)}) collective-permute-start(bf16[2,16,2048]{2,1,0:T(8,128)(2,1)S(1)} %get-tuple-element.30), channel_id=1, source_target_pairs={{0,4},{1,5},{2,6},{3,7},{4,0},{5,1},{6,2},{7,3},{8,12},{9,13},{10,... | collective-permute-start | bytes 393224 | tf_op jit(solution)/shard_map/ppermute | solution.py:464
  220.3 18.2 %collective-permute-start.6 = (bf16[2,16,2048]{2,1,0:T(8,128)(2,1)S(1)}, bf16[2,16,2048]{2,1,0:T(8,128)(2,1)S(1)}, u32[]{:S(2)}, u32[]{:S(2)}) collective-permute-start(bf16[2,16,2048]{2,1,0:T(8,128)(2,1)S(1)} %get-tuple-element.25), channel_id=1, source_target_pairs={{0,248},{8,240},{16,232},{24,224},{32,216},{40,208},{48,200},{56,1... | collective-permute-start | bytes 393224 | tf_op jit(solution)/shard_map/ppermute | solution.py:465
  220.4 18.1 %collective-permute-start.7 = (bf16[2,16,2048]{2,1,0:T(8,128)(2,1)S(1)}, bf16[2,16,2048]{2,1,0:T(8,128)(2,1)S(1)}, u32[]{:S(2)}, u32[]{:S(2)}) collective-permute-start(bf16[2,16,2048]{2,1,0:T(8,128)(2,1)S(1)} %get-tuple-element.25), channel_id=1, source_target_pairs={{0,252},{1,253},{2,254},{3,255},{4,248},{5,249},{6,250},{7,251},{8... | collective-permute-start | bytes 393224 | tf_op jit(solution)/shard_map/ppermute | solution.py:466
  225.0 13.6 %collective-permute-start.5 = (bf16[2,16,2048]{2,1,0:T(8,128)(2,1)S(1)}, bf16[2,16,2048]{2,1,0:T(8,128)(2,1)S(1)}, u32[]{:S(2)}, u32[]{:S(2)}) collective-permute-start(bf16[2,16,2048]{2,1,0:T(8,128)(2,1)S(1)} %get-tuple-element.26), channel_id=1, source_target_pairs={{0,4},{1,5},{2,6},{3,7},{4,0},{5,1},{6,2},{7,3},{8,12},{9,13},{10,... | collective-permute-start | bytes 393224 | tf_op jit(solution)/shard_map/ppermute | solution.py:464
  265.8 17.7 %all-to-all-start.5 = ((bf16[4,64,2048]{2,1,0:T(8,128)(2,1)}), bf16[4,64,2048]{2,1,0:T(8,128)(2,1)S(1)}, u32[]{:S(2)}, u32[]{:S(2)}) async-start(bf16[4,64,2048]{2,1,0:T(8,128)(2,1)} %bitcast.83), calls=%async_computation.5 | async-start | bytes 2097152 | tf_op jit(solution)/shard_map/all_to_all | solution.py:402
  284.0 15.6 %collective-permute-start.9 = (bf16[64,2048]{1,0:T(8,128)(2,1)S(1)}, bf16[64,2048]{1,0:T(8,128)(2,1)S(1)}, u32[]{:S(2)}, u32[]{:S(2)}) collective-permute-start(bf16[64,2048]{1,0:T(8,128)(2,1)S(1)} %shard_map.143), channel_id=1, source_target_pairs={{0,4},{1,5},{2,6},{3,7},{4,0},{5,1},{6,2},{7,3},{8,12},{9,13},{10,... | collective-permute-start | bytes 786440 | tf_op jit(solution)/shard_map/ppermute | solution.py:514
Sparse Core Ops, SparseCore 0:
  9.2 77.3 all-gather.2
  90.3 68.4 all-gather.4

commit v4 on v3

--- a/solution.py
+++ b/solution.py
@@ -98,30 +98,25 @@
     rows = devices * tile
     span = half // devices
     block = 2 * half
-    chunks = sems.shape[0]
-    ctx = kv_ref.shape[0] // block
+    chunks = sems.shape[1]
+    ctx = kv_ref.shape[0]
     per = ctx // chunks
     place = place_ref[0]
     pair = 4
     cols = pair * rows
     longest = jnp.maximum(place, ctx - 1 - place)
 
-    def chunk_wait(at):
-        piece = pl.ds(pl.multiple_of(at * per * block, block), per * block)
-        pltpu.make_async_copy(kv_hbm.at[piece], kv_ref.at[piece], sems.at[at]).wait()
+    def chunk_copies(at):
+        for job, first in enumerate((at * per, ctx - (at + 1) * per)):
+            piece = (pl.ds(first, per), job)
+            yield pltpu.make_async_copy(kv_hbm.at[piece], kv_ref.at[piece], sems.at[job, at])
 
     wo_copy = pltpu.make_async_copy(w_hbm.at[:, feats : 2 * feats], wo_ref, wo_sem)
     for at in range(chunks):
         @pl.when(at * per <= longest)
         def _(at=at):
-            for one in range(at * per, (at + 1) * per):
-                first = pl.ds(one * block, half)
-                pltpu.make_async_copy(kv_hbm.at[first], kv_ref.at[first], sems.at[at]).start()
-                pltpu.make_async_copy(
-                    kv_hbm.at[pl.ds((ctx - 1 - one) * block + half, half)],
-                    kv_ref.at[pl.ds(one * block + half, half)],
-                    sems.at[at],
-                ).start()
+            for copy in chunk_copies(at):
+                copy.start()
 
     wo_copy.start()
 
@@ -153,15 +148,18 @@
 
             def product(item):
                 start, group = item
-                keys = kv_ref[pl.ds(pl.multiple_of(start, half), count), :head]
+                keys = jnp.concatenate(
+                    [kv_ref[start, 0, :, :head], kv_ref[ctx - 1 - start, 1, :, :head]], axis=0
+                )
                 queries = qt_ref[job, :, group * cols : (group + 1) * cols]
                 return jnp.dot(keys, queries, preferred_element_type=F32)
 
             def collect(start, group, weights, decay):
                 values = jnp.concatenate(
                     [
-                        kv_ref[pl.ds(pl.multiple_of(start + i * head, head), head), head:]
-                        for i in range(count // head)
+                        kv_ref[spot, job, i * head : (i + 1) * head, head:]
+                        for job, spot in enumerate((start, ctx - 1 - start))
+                        for i in range(half // head)
                     ],
                     axis=1,
                 )
@@ -199,11 +197,12 @@
         def arrive(at):
             @pl.when(turn == 0)
             def _():
-                chunk_wait(at)
+                for copy in chunk_copies(at):
+                    copy.wait()
 
         def whole_chunk(at, state):
             arrive(at)
-            return steps([(at * per + i) * block for i in range(per)], state)
+            return steps([at * per + i for i in range(per)], state)
 
         acc_ref[...] = jnp.zeros_like(acc_ref)
         state = (jnp.full((1, cols), -1e30, F32), jnp.zeros((8, cols), F32)) * groups
@@ -212,7 +211,7 @@
         arrive(full)
         tails = [
             lambda now, left=left: steps(
-                [(blocks - left + i) * block for i in range(left + 1)], now, masked=True
+                [blocks - left + i for i in range(left + 1)], now, masked=True
             )
             for left in range(per)
         ]
@@ -250,8 +249,9 @@
     tile = half // (2 * ring) // parts
     rows = tile * 2 * ring
     ctx = kv.shape[0] // (2 * half)
+    kv = kv.reshape(ctx, 2, half, kv.shape[1])
     chunks = max(1, ctx // 4)
-    flops = 8 * kv.shape[0] * rows * feats
+    flops = 16 * ctx * half * rows * feats
     return pl.pallas_call(
         functools.partial(attention_kernel, math.log2(math.e) / math.sqrt(head), part),
         grid_spec=pltpu.PrefetchScalarGridSpec(
@@ -269,7 +269,7 @@
                 pltpu.VMEM((2, head, rows * feats // head), BF16),
                 pltpu.VMEM((head, rows * feats // head), F32),
                 pltpu.VMEM((rows, feats), BF16),
-                pltpu.SemaphoreType.DMA((chunks,)),
+                pltpu.SemaphoreType.DMA((2, chunks)),
                 pltpu.SemaphoreType.DMA,
             ],
         ),
@@ -299,49 +299,86 @@
     sent_ref[...] = jnp.dot(chosen_ref[...], rows, preferred_element_type=F32).astype(BF16)
 
 
-def expert_kernel(rows_ref, gate_ref, up_ref, down_ref, out_ref, total_ref):
-    step = pl.program_id(0)
-    gate = jnp.dot(rows_ref[...], gate_ref[...], preferred_element_type=F32)
-    up = jnp.dot(rows_ref[...], up_ref[...], preferred_element_type=F32)
+def expert_kernel(
+    place_ref, rows_ref, gate_hbm, up_hbm, down_hbm, mine_ref, theirs_ref,
+    gate_ref, up_ref, down_ref, total_ref, sems,
+):
+    count, width = rows_ref.shape
+    pieces = sems.shape[1]
+    copies = []
+    for kind, (source, target) in enumerate(
+        ((gate_hbm, gate_ref), (up_hbm, up_ref), (down_hbm, down_ref))
+    ):
+        step = target.shape[0] // pieces
+        copies.append(
+            [
+                pltpu.make_async_copy(
+                    source.at[pl.ds(at * step, step)],
+                    target.at[pl.ds(at * step, step)],
+                    sems.at[kind, at],
+                )
+                for at in range(pieces)
+            ]
+        )
+    order = [copies[kind][at] for at in range(pieces) for kind in range(2)] + copies[2]
+    ahead = 6
+    for copy in order[:ahead]:
+        copy.start()
+
+    def arrive(at):
+        order[at].wait()
+        if at + ahead < len(order):
+            order[at + ahead].start()
+
+    step = width // pieces
+    gate = up = 0.0
+    for at in range(pieces):
+        part = slice(at * step, (at + 1) * step)
+        arrive(2 * at)
+        gate += jnp.dot(rows_ref[:, part], gate_ref[part], preferred_element_type=F32)
+        arrive(2 * at + 1)
+        up += jnp.dot(rows_ref[:, part], up_ref[part], preferred_element_type=F32)
     hidden = (gate / (1.0 + jnp.exp(-gate)) * up).astype(BF16)
-    share = jnp.dot(hidden, down_ref[...], preferred_element_type=F32)
-
-    @pl.when(step == 0)
-    def _():
-        total_ref[...] = share
-
-    @pl.when(step > 0)
-    def _():
-        total_ref[...] += share
-
-    @pl.when(step == pl.num_programs(0) - 1)
-    def _():
-        out_ref[...] = total_ref[...].astype(BF16)
-
-
-def run_experts(rows, gate_weight, up_weight, down_weight):
+    for at in range(2 * pieces, 3 * pieces):
+        arrive(at)
+    total_ref[...] = jnp.dot(hidden, down_ref[...], preferred_element_type=F32)
+    capacity = mine_ref.shape[1]
+    for near in range(mine_ref.shape[0]):
+        for target, side in ((mine_ref, place_ref[0]), (theirs_ref, 1 - place_ref[0])):
+            start = pl.multiple_of((near * 2 + side) * capacity, capacity)
+            target[near] = total_ref[pl.ds(start, capacity)].astype(BF16)
+
+
+def run_experts(place, rows, gate_weight, up_weight, down_weight, ring):
     count, width = rows.shape
     inner = gate_weight.shape[1]
-    piece = math.gcd(inner, 256)
+    pieces = 4
+    shape = (ring, count // ring // 2, width)
+    hbm = pl.BlockSpec(memory_space=pltpu.HBM)
+    whole = pl.BlockSpec(shape, lambda i, p: (0, 0, 0))
     return pl.pallas_call(
         expert_kernel,
-        grid=(inner // piece,),
-        in_specs=[
-            pl.BlockSpec((count, width), lambda i: (0, 0)),
-            pl.BlockSpec((width, piece), lambda i: (0, i)),
-            pl.BlockSpec((width, piece), lambda i: (0, i)),
-            pl.BlockSpec((piece, width), lambda i: (i, 0)),
-        ],
-        out_specs=pl.BlockSpec((count, width), lambda i: (0, 0)),
-        scratch_shapes=[pltpu.VMEM((count, width), F32)],
-        out_shape=jax.ShapeDtypeStruct((count, width), BF16),
+        grid_spec=pltpu.PrefetchScalarGridSpec(
+            num_scalar_prefetch=1,
+            grid=(1,),
+            in_specs=[pl.BlockSpec((count, width), lambda i, p: (0, 0)), hbm, hbm, hbm],
+            out_specs=(whole, whole),
+            scratch_shapes=[
+                pltpu.VMEM((width, inner), BF16),
+                pltpu.VMEM((width, inner), BF16),
+                pltpu.VMEM((inner, width), BF16),
+                pltpu.VMEM((count, width), F32),
+                pltpu.SemaphoreType.DMA((3, pieces)),
+            ],
+        ),
+        out_shape=(jax.ShapeDtypeStruct(shape, BF16),) * 2,
         compiler_params=params(58),
         cost_estimate=pl.CostEstimate(
             flops=6 * count * width * inner,
             bytes_accessed=6 * width * inner,
             transcendentals=count * inner,
         ),
-    )(rows, gate_weight, up_weight, down_weight)
+    )(place, rows, gate_weight, up_weight, down_weight)
 
 
 def combine_kernel(back_ref, rows_ref, weight_ref, base_ref, out_ref):
@@ -504,15 +541,19 @@
     mixed_both = mixed_both.reshape(2, 2, half_tile, width)
     mixed = lax.dynamic_index_in_dim(mixed_both, far, 1, keepdims=False).reshape(tok_rows, width)
     arrived = over_ring(sent.reshape(ring, 2 * capacity, width)).reshape(-1, width)
-    done = run_experts(arrived, gate_weight[0], up_weight[0], expert_down_matrix[0])
-    back = over_ring(done.reshape(ring, 2 * capacity, width)).reshape(-1, width)
+    own_done, far_done = run_experts(
+        far_index, arrived, gate_weight[0], up_weight[0], expert_down_matrix[0], ring
+    )
     theirs, mine = (
-        [lax.dynamic_index_in_dim(a, side, 0, keepdims=False) for a in (rows_of, route_weight)]
+        [lax.dynamic_index_in_dim(a, side, 0, keepdims=False) for a in (both_slots, route_weight)]
         for side in (1 - far, far)
     )
-    given = combine(back, *theirs, jnp.zeros((tok_rows, width), F32), BF16)
+    far_back = over_ring(far_done).reshape(-1, width)
+    given = combine(far_back, *theirs, jnp.zeros((tok_rows, width), F32), BF16)
     returned = lax.ppermute(given, "exp", flip)
-    total = combine(back, *mine, mixed, F32)
+    given, own_done = lax.optimization_barrier((given, own_done))
+    own_back = over_ring(own_done).reshape(-1, width)
+    total = combine(own_back, *mine, mixed, F32)
     return (total + returned.astype(F32)).astype(BF16)
 
 

time: 308 us -> 307 us (level)
  blocking collectives: 18.5 us -> 0 us
  waiting for transfers between devices: 156 us -> 164 us
  starting transfers between devices: 53.7 us -> 61.3 us
    all_to_all x1 -> x0, blocking collectives: 18.5 us -> none  [over_ring(): lax.all_to_all(parts, 'exp', 0, 0, tiled=True, axis_index_groups=rings)]
    all_to_all x5 -> x7, waiting for transfers between devices: 32.4 us -> 47.7 us  [over_ring(): lax.all_to_all(parts, 'exp', 0, 0, tiled=True, axis_index_groups=rings)]
    all_to_all x5 -> x7, starting transfers between devices: 21.4 us -> 28.8 us  [over_ring(): lax.all_to_all(parts, 'exp', 0, 0, tiled=True, axis_index_groups=rings)]
    ppermute x1, waiting for transfers between devices: 12.9 us -> 6.31 us  [shards(): returned = lax.ppermute(given, 'exp', flip)]
  transfers between devices with their start and end apart: 17 -> 19, of which waited for: 10 -> 12; matrix products, arithmetic and copies ran while one was open for 3% -> 3% of each run, Pallas kernels for 8% -> 8%
where the time goes in v4:
time: 307 us; the launch traced here: 306 us
  waiting for transfers between devices  164 us (53%)
  starting transfers between devices  61.3 us (20%)
  Pallas kernels  54.7 us (18%)
  between operations  13.8 us (4%)
  local copies, waits for them, and re-layouts  6.88 us (2%)
  other arithmetic  5.23 us (2%)
    all_gather x1, waiting for transfers between devices, shards(): kv_all = lax.all_gather(kv, 'ctx', axis=0, tiled=True)  53.8 us
    all_to_all x7, waiting for transfers between devices, over_ring(): lax.all_to_all(parts, 'exp', 0, 0, tiled=True, axis_index_groups=rings)  47.7 us
    pallas_call x2, Pallas kernels, attend(): pl.pallas_call(functools.partial(attention_kernel, math.log2(math.e) / ma...  36.6 us
    all_to_all x7, starting transfers between devices, over_ring(): lax.all_to_all(parts, 'exp', 0, 0, tiled=True, axis_index_groups=rings)  28.8 us
    all_gather x1, waiting for transfers between devices, shards(): weights = lax.all_gather(packed, 'ctx', axis=0, tiled=True)  27.4 us
    ppermute x1, waiting for transfers between devices, shards(): flipped = lax.ppermute(worked, 'exp', flip)  11.2 us
    ppermute x2, waiting for transfers between devices, shards(): lax.ppermute(rounded[0], 'exp', flip)  11 us
    ppermute x2, starting transfers between devices, shards(): lax.ppermute(rounded[1], ('ctx', 'exp'), cross)  8.13 us
  transfers between devices with their start and end apart: 19, of which 12 were waited for; matrix products, arithmetic and copies ran while one was open for 3% of the time, Pallas kernels for 8%

profile of v4, /device:TPU:8, one launch (start us, length us, event | category | flops | bytes accessed | tf_op | source)
XLA Modules:
  0.0 306.0 jit_solution(7182586578843425422)
XLA Ops:
  9.8 5.2 %collective-permute-start = (bf16[32,2048]{1,0:T(8,128)(2,1)S(1)}, bf16[32,2048]{1,0:T(8,128)(2,1)S(1)}, u32[]{:S(2)}, u32[]{:S(2)}) collective-permute-start(bf16[32,2048]{1,0:T(8,128)(2,1)S(1)} %get-tuple-element.38), channel_id=1, source_target_pairs={{0,248},{8,240},{16,232},{24,224},{32,216},{40,208},{48,200},{56,1... | collective-permute-start | bytes 393224 | tf_op jit(solution)/shard_map/ppermute | solution.py:456
  15.7 3.2 %collective-permute-done = bf16[32,2048]{1,0:T(8,128)(2,1)S(1)} collective-permute-done((bf16[32,2048]{1,0:T(8,128)(2,1)S(1)}, bf16[32,2048]{1,0:T(8,128)(2,1)S(1)}, u32[]{:S(2)}, u32[]{:S(2)}) %collective-permute-start) | collective-permute-done | bytes 131104 | tf_op jit(solution)/shard_map/ppermute | solution.py:456
  20.4 4.3 %all-to-all-start = ((bf16[4,64,2048]{2,1,0:T(8,128)(2,1)}), bf16[4,64,2048]{2,1,0:T(8,128)(2,1)S(1)}, u32[]{:S(2)}, u32[]{:S(2)}) async-start(bf16[4,64,2048]{2,1,0:T(8,128)(2,1)} %broadcast_in_dim.61), calls=%async_computation | async-start | bytes 2097152 | tf_op jit(solution)/shard_map/all_to_all | solution.py:439
  24.7 6.8 %collective-permute-start.1 = (bf16[64,2048]{1,0:T(8,128)(2,1)S(1)}, bf16[64,2048]{1,0:T(8,128)(2,1)S(1)}, u32[]{:S(2)}, u32[]{:S(2)}) collective-permute-start(bf16[64,2048]{1,0:T(8,128)(2,1)S(1)} %fusion.2), channel_id=1, source_target_pairs={{0,4},{1,5},{2,6},{3,7},{4,0},{5,1},{6,2},{7,3},{8,12},{9,13},{10,... | collective-permute-start | bytes 786440 | tf_op jit(solution)/shard_map/ppermute | solution.py:461
  31.4 11.2 %collective-permute-done.1 = bf16[64,2048]{1,0:T(8,128)(2,1)S(1)} collective-permute-done((bf16[64,2048]{1,0:T(8,128)(2,1)S(1)}, bf16[64,2048]{1,0:T(8,128)(2,1)S(1)}, u32[]{:S(2)}, u32[]{:S(2)}) %collective-permute-start.1) | collective-permute-done | bytes 262176 | tf_op jit(solution)/shard_map/ppermute | solution.py:461
  43.8 4.5 %all-to-all-start.1 = ((bf16[4,64,2048]{2,1,0:T(8,128)(2,1)}), bf16[4,64,2048]{2,1,0:T(8,128)(2,1)S(1)}, u32[]{:S(2)}, u32[]{:S(2)}) async-start(bf16[4,64,2048]{2,1,0:T(8,128)(2,1)} %broadcast_in_dim.62), calls=%async_computation.1 | async-start | bytes 2097152 | tf_op jit(solution)/shard_map/all_to_all | solution.py:439
  48.4 10.9 %all-to-all-done.1 = bf16[4,64,2048]{2,1,0:T(8,128)(2,1)S(1)} async-done(((bf16[4,64,2048]{2,1,0:T(8,128)(2,1)}), bf16[4,64,2048]{2,1,0:T(8,128)(2,1)S(1)}, u32[]{:S(2)}, u32[]{:S(2)}) %all-to-all-start.1) | async-done | bytes 1048608 | tf_op jit(solution)/shard_map/all_to_all | solution.py:439
  59.2 27.4 %all-gather.3.cloned.1.call-done.w_ref.w_hbm = bf16[2048,1280]{1,0:T(8,128)(2,1)} async-done(((bf16[64,1280]{1,0:T(8,128)(2,1)}), bf16[2048,1280]{1,0:T(8,128)(2,1)}) %all-gather.3.cloned.1.call-update) | async-done | bytes 5242896 | tf_op jit(solution)/shard_map/all_gather | solution.py:454
  86.7 3.5 %shard_map.137 = bf16[512,256]{1,0:T(8,128)(2,1)} custom-call(s32[1]{0:T(128)} %bitcast.place_ref, bf16[256,2048]{1,0:T(8,128)(2,1)} %bitcast.79, bf16[256,2048]{1,0:T(8,128)(2,1)} %bitcast.81, bf16[2048,1280]{1,0:T(8,128)(2,1)} %all-gather.3.cloned.1.call-done.w_ref.w_hbm, bf16[1,128]{1,0:T(2,128)(2,1)} %bitcast.96), custom_call_target="tpu_custom_call" | custom-call | flops 536870912 | bytes 8388608 | tf_op jit(solution)/shard_map/pallas_call | solution.py:69
  90.2 4.1 %collective-permute-start.8 = (s32[64,4]{0,1:T(4,128)S(1)}, s32[64,4]{0,1:T(4,128)S(1)}, u32[]{:S(2)}, u32[]{:S(2)}) collective-permute-start(s32[64,4]{0,1:T(4,128)S(1)} %get-tuple-element.48), channel_id=1, source_target_pairs={{0,4},{1,5},{2,6},{3,7},{4,0},{5,1},{6,2},{7,3},{8,12},{9,13},{10,... | collective-permute-start | bytes 3080 | tf_op jit(solution)/shard_map/ppermute | solution.py:460
  94.3 3.4 %collective-permute-done.8 = s32[64,4]{0,1:T(4,128)S(1)} collective-permute-done((s32[64,4]{0,1:T(4,128)S(1)}, s32[64,4]{0,1:T(4,128)S(1)}, u32[]{:S(2)}, u32[]{:S(2)}) %collective-permute-start.8) | collective-permute-done | bytes 1056 | tf_op jit(solution)/shard_map/ppermute | solution.py:460
  100.3 4.6 %shard_map.136.q_ref = bf16[2,256,512]{2,1,0:T(8,128)(2,1)} custom-call(s32[1]{0:T(128)} %bitcast.place_ref, bf16[256,2048]{1,0:T(8,128)(2,1)} %bitcast.80, bf16[256,2048]{1,0:T(8,128)(2,1)} %bitcast.82, bf16[2048,1280]{1,0:T(8,128)(2,1)} %all-gather.3.cloned.1.call-done.w_ref.w_hbm, bf16[1,128]{1,0:T(2,128)(2,1)} %bitcast.97), custom_call_target="tpu_custom_call" | custom-call | flops 1073741824 | bytes 8388608 | tf_op jit(solution)/shard_map/pallas_call | solution.py:69
  104.9 53.8 %all-gather.5.cloned.1.call-done = bf16[16384,256]{1,0:T(8,128)(2,1)} async-done(((bf16[512,256]{1,0:T(8,128)(2,1)}), bf16[16384,256]{1,0:T(8,128)(2,1)}) %all-gather.5.cloned.1.call-update) | async-done | bytes 8388624 | tf_op jit(solution)/shard_map/all_gather | solution.py:478
  158.7 18.3 %shard_map.138 = bf16[4,2,2,16,2048]{4,3,2,1,0:T(8,128)(2,1)} custom-call(s32[1]{0:T(128)} %bitcast.1.place_ref, bf16[2,256,512]{2,1,0:T(8,128)(2,1)} %shard_map.136.q_ref, bf16[32,2,256,256]{3,2,1,0:T(8,128)(2,1)} %bitcast.98, bf16[2048,1280]{1,0:T(8,128)(2,1)} %all-gather.3.cloned.1.call-done.w_ref.w_hbm), custom_call_target="tpu_custom_call" | custom-call | flops 8589934592 | bytes 16777216 | tf_op jit(solution)/shard_map/pallas_call | solution.py:255
  177.0 4.5 %all-to-all-start.2 = ((bf16[4,2,2,16,2048]{4,3,2,1,0:T(8,128)(2,1)}), bf16[4,2,2,16,2048]{4,3,2,1,0:T(8,128)(2,1)S(1)}, u32[]{:S(2)}, u32[]{:S(2)}) async-start(bf16[4,2,2,16,2048]{4,3,2,1,0:T(8,128)(2,1)} %shard_map.138), calls=%async_computation.2 | async-start | bytes 2097152 | tf_op jit(solution)/shard_map/all_to_all | solution.py:439
  181.5 18.3 %shard_map.139 = bf16[4,2,2,16,2048]{4,3,2,1,0:T(8,128)(2,1)} custom-call(s32[1]{0:T(128)} %bitcast.1.place_ref, bf16[2,256,512]{2,1,0:T(8,128)(2,1)} %shard_map.136.q_ref, bf16[32,2,256,256]{3,2,1,0:T(8,128)(2,1)} %bitcast.99, bf16[2048,1280]{1,0:T(8,128)(2,1)} %all-gather.3.cloned.1.call-done.w_ref.w_hbm), custom_call_target="tpu_custom_call" | custom-call | flops 8589934592 | bytes 16777216 | tf_op jit(solution)/shard_map/pallas_call | solution.py:255
  200.1 4.8 %all-to-all-start.3 = ((bf16[4,2,2,16,2048]{4,3,2,1,0:T(8,128)(2,1)}), bf16[4,2,2,16,2048]{4,3,2,1,0:T(8,128)(2,1)S(1)}, u32[]{:S(2)}, u32[]{:S(2)}) async-start(bf16[4,2,2,16,2048]{4,3,2,1,0:T(8,128)(2,1)} %shard_map.139), calls=%async_computation.3 | async-start | bytes 2097152 | tf_op jit(solution)/shard_map/all_to_all | solution.py:439
  206.1 3.5 %collective-permute-start.4 = (bf16[2,16,2048]{2,1,0:T(8,128)(2,1)S(1)}, bf16[2,16,2048]{2,1,0:T(8,128)(2,1)S(1)}, u32[]{:S(2)}, u32[]{:S(2)}) collective-permute-start(bf16[2,16,2048]{2,1,0:T(8,128)(2,1)S(1)} %get-tuple-element.35), channel_id=1, source_target_pairs={{0,252},{1,253},{2,254},{3,255},{4,248},{5,249},{6,250},{7,251},{8... | collective-permute-start | bytes 393224 | tf_op jit(solution)/shard_map/ppermute | solution.py:503
  209.6 2.5 collective-permute-start.2
  212.1 7.9 %all-to-all-done.3 = bf16[4,2,2,16,2048]{4,3,2,1,0:T(8,128)(2,1)S(1)} async-done(((bf16[4,2,2,16,2048]{4,3,2,1,0:T(8,128)(2,1)}), bf16[4,2,2,16,2048]{4,3,2,1,0:T(8,128)(2,1)S(1)}, u32[]{:S(2)}, u32[]{:S(2)}) %all-to-all-start.3) | async-done | bytes 1048608 | tf_op jit(solution)/shard_map/all_to_all | solution.py:439
  220.5 4.6 %collective-permute-start.7 = (bf16[2,16,2048]{2,1,0:T(8,128)(2,1)S(1)}, bf16[2,16,2048]{2,1,0:T(8,128)(2,1)S(1)}, u32[]{:S(2)}, u32[]{:S(2)}) collective-permute-start(bf16[2,16,2048]{2,1,0:T(8,128)(2,1)S(1)} %get-tuple-element.31), channel_id=1, source_target_pairs={{0,252},{1,253},{2,254},{3,255},{4,248},{5,249},{6,250},{7,251},{8... | collective-permute-start | bytes 393224 | tf_op jit(solution)/shard_map/ppermute | solution.py:503
  225.1 2.5 collective-permute-start.5
  227.6 11.0 %collective-permute-done.5.refs_5_ = bf16[2,16,2048]{2,1,0:T(8,128)(2,1)S(1)} collective-permute-done((bf16[2,16,2048]{2,1,0:T(8,128)(2,1)S(1)}, bf16[2,16,2048]{2,1,0:T(8,128)(2,1)S(1)}, u32[]{:S(2)}, u32[]{:S(2)}) %collective-permute-start.5) | collective-permute-done | bytes 131104 | tf_op jit(solution)/shard_map/ppermute | solution.py:501
  240.4 3.7 %all-to-all-start.4 = ((bf16[4,64,2048]{2,1,0:T(8,128)(2,1)}), bf16[4,64,2048]{2,1,0:T(8,128)(2,1)S(1)}, u32[]{:S(2)}, u32[]{:S(2)}) async-start(bf16[4,64,2048]{2,1,0:T(8,128)(2,1)} %bitcast.23), calls=%async_computation.4 | async-start | bytes 2097152 | tf_op jit(solution)/shard_map/all_to_all | solution.py:439
  244.1 14.9 %all-to-all-done.4 = bf16[4,64,2048]{2,1,0:T(8,128)(2,1)S(1)} async-done(((bf16[4,64,2048]{2,1,0:T(8,128)(2,1)}), bf16[4,64,2048]{2,1,0:T(8,128)(2,1)S(1)}, u32[]{:S(2)}, u32[]{:S(2)}) %all-to-all-start.4) | async-done | bytes 1048608 | tf_op jit(solution)/shard_map/all_to_all | solution.py:439
  260.0 7.7 %shard_map.141 = (bf16[4,32,2048]{2,1,0:T(8,128)(2,1)}, bf16[4,32,2048]{2,1,0:T(8,128)(2,1)}) custom-call(s32[1]{0:T(128)} %bitcast.place_ref, bf16[256,2048]{1,0:T(8,128)(2,1)} %bitcast.83, bf16[2048,768]{1,0:T(8,128)(2,1)} %bitcast.84, bf16[2048,768]{1,0:T(8,128)(2,1)} %bitcast.85, bf16[768,2048]{1,0:T(8,128)(2,1)} %bitcast.86), custom_call_target="tpu_custom_call" | custom-call | flops 2415919104 | bytes 9437184 | tf_op jit(solution)/shard_map/pallas_call | solution.py:359
  267.7 3.5 %all-to-all-start.5 = ((bf16[4,32,2048]{2,1,0:T(8,128)(2,1)}), bf16[4,32,2048]{2,1,0:T(8,128)(2,1)S(1)}, u32[]{:S(2)}, u32[]{:S(2)}) async-start(bf16[4,32,2048]{2,1,0:T(8,128)(2,1)} %get-tuple-element.17), calls=%async_computation.5 | async-start | bytes 1048576 | tf_op jit(solution)/shard_map/all_to_all | solution.py:439
  271.7 8.1 %all-to-all-done.5 = bf16[4,32,2048]{2,1,0:T(8,128)(2,1)S(1)} async-done(((bf16[4,32,2048]{2,1,0:T(8,128)(2,1)}), bf16[4,32,2048]{2,1,0:T(8,128)(2,1)S(1)}, u32[]{:S(2)}, u32[]{:S(2)}) %all-to-all-start.5) | async-done | bytes 524320 | tf_op jit(solution)/shard_map/all_to_all | solution.py:439
  280.2 3.5 %all-to-all-start.6 = ((bf16[4,32,2048]{2,1,0:T(8,128)(2,1)}), bf16[4,32,2048]{2,1,0:T(8,128)(2,1)S(1)}, u32[]{:S(2)}, u32[]{:S(2)}) async-start(bf16[4,32,2048]{2,1,0:T(8,128)(2,1)} %get-tuple-element.19), calls=%async_computation.6 | async-start | bytes 1048576 | tf_op jit(solution)/shard_map/all_to_all | solution.py:439
  283.7 2.1 collective-permute-start.9
  285.8 5.9 %all-to-all-done.6 = bf16[4,32,2048]{2,1,0:T(8,128)(2,1)S(1)} async-done(((bf16[4,32,2048]{2,1,0:T(8,128)(2,1)}), bf16[4,32,2048]{2,1,0:T(8,128)(2,1)S(1)}, u32[]{:S(2)}, u32[]{:S(2)}) %all-to-all-start.6) | async-done | bytes 524320 | tf_op jit(solution)/shard_map/all_to_all | solution.py:439
  292.1 6.3 %collective-permute-done.9 = bf16[64,2048]{1,0:T(8,128)(2,1)S(1)} collective-permute-done((bf16[64,2048]{1,0:T(8,128)(2,1)S(1)}, bf16[64,2048]{1,0:T(8,128)(2,1)S(1)}, u32[]{:S(2)}, u32[]{:S(2)}) %collective-permute-start.9) | collective-permute-done | bytes 262176 | tf_op jit(solution)/shard_map/ppermute | solution.py:553
  (88 shorter events, 15.8 us)
Async XLA Ops:
  6.5 80.1 %all-gather.3.cloned.1.call-start = ((), (), s32[]{:S(2)}) async-start(), calls=%async_computation.7 | async-start | bytes 5406720 | tf_op jit(solution)/shard_map/all_gather | solution.py:454
  9.8 9.1 %collective-permute-start = (bf16[32,2048]{1,0:T(8,128)(2,1)S(1)}, bf16[32,2048]{1,0:T(8,128)(2,1)S(1)}, u32[]{:S(2)}, u32[]{:S(2)}) collective-permute-start(bf16[32,2048]{1,0:T(8,128)(2,1)S(1)} %get-tuple-element.38), channel_id=1, source_target_pairs={{0,248},{8,240},{16,232},{24,224},{32,216},{40,208},{48,200},{56,1... | collective-permute-start | bytes 393224 | tf_op jit(solution)/shard_map/ppermute | solution.py:456
  20.4 22.3 %all-to-all-start = ((bf16[4,64,2048]{2,1,0:T(8,128)(2,1)}), bf16[4,64,2048]{2,1,0:T(8,128)(2,1)S(1)}, u32[]{:S(2)}, u32[]{:S(2)}) async-start(bf16[4,64,2048]{2,1,0:T(8,128)(2,1)} %broadcast_in_dim.61), calls=%async_computation | async-start | bytes 2097152 | tf_op jit(solution)/shard_map/all_to_all | solution.py:439
  24.7 18.0 %collective-permute-start.1 = (bf16[64,2048]{1,0:T(8,128)(2,1)S(1)}, bf16[64,2048]{1,0:T(8,128)(2,1)S(1)}, u32[]{:S(2)}, u32[]{:S(2)}) collective-permute-start(bf16[64,2048]{1,0:T(8,128)(2,1)S(1)} %fusion.2), channel_id=1, source_target_pairs={{0,4},{1,5},{2,6},{3,7},{4,0},{5,1},{6,2},{7,3},{8,12},{9,13},{10,... | collective-permute-start | bytes 786440 | tf_op jit(solution)/shard_map/ppermute | solution.py:461
  42.6 44.0 %copy-start = (bf16[4,64,2048]{2,1,0:T(8,128)(2,1)}, bf16[4,64,2048]{2,1,0:T(8,128)(2,1)S(1)}, u32[]{:S(2)}) copy-start(bf16[4,64,2048]{2,1,0:T(8,128)(2,1)S(1)} %all-to-all-done) | copy-start | bytes 3145732
  43.8 15.4 %all-to-all-start.1 = ((bf16[4,64,2048]{2,1,0:T(8,128)(2,1)}), bf16[4,64,2048]{2,1,0:T(8,128)(2,1)S(1)}, u32[]{:S(2)}, u32[]{:S(2)}) async-start(bf16[4,64,2048]{2,1,0:T(8,128)(2,1)} %broadcast_in_dim.62), calls=%async_computation.1 | async-start | bytes 2097152 | tf_op jit(solution)/shard_map/all_to_all | solution.py:439
  48.4 110.4 %all-gather.5.cloned.1.call-start = ((), (), s32[]{:S(2)}) async-start(), calls=%async_computation.8 | async-start | bytes 8650752 | tf_op jit(solution)/shard_map/all_gather | solution.py:478
  59.2 27.4 %copy-start.1 = (bf16[4,64,2048]{2,1,0:T(8,128)(2,1)}, bf16[4,64,2048]{2,1,0:T(8,128)(2,1)S(1)}, u32[]{:S(2)}) copy-start(bf16[4,64,2048]{2,1,0:T(8,128)(2,1)S(1)} %all-to-all-done.1) | copy-start | bytes 3145732
  86.6 3.5 %copy-start.4 = (s32[64,2]{0,1:T(2,128)S(1)}, s32[64,2]{0,1:T(2,128)}, u32[]{:S(2)}) copy-start(s32[64,2]{0,1:T(2,128)} %param.24) | copy-start | bytes 1540
  86.6 3.5 %copy-start.5 = (s32[64,2]{0,1:T(2,128)S(1)}, s32[64,2]{0,1:T(2,128)}, u32[]{:S(2)}) copy-start(s32[64,2]{0,1:T(2,128)} %param.23) | copy-start | bytes 1540
  86.7 7.7 %copy-start.3 = (bf16[2048]{0:T(1024)(128)(2,1)S(1)}, bf16[2048]{0:T(1024)(128)(2,1)}, u32[]{:S(2)}) copy-start(bf16[2048]{0:T(1024)(128)(2,1)} %param.22) | copy-start | bytes 12292
  90.2 7.6 %collective-permute-start.8 = (s32[64,4]{0,1:T(4,128)S(1)}, s32[64,4]{0,1:T(4,128)S(1)}, u32[]{:S(2)}, u32[]{:S(2)}) collective-permute-start(s32[64,4]{0,1:T(4,128)S(1)} %get-tuple-element.48), channel_id=1, source_target_pairs={{0,4},{1,5},{2,6},{3,7},{4,0},{5,1},{6,2},{7,3},{8,12},{9,13},{10,... | collective-permute-start | bytes 3080 | tf_op jit(solution)/shard_map/ppermute | solution.py:460
  177.0 22.7 %all-to-all-start.2 = ((bf16[4,2,2,16,2048]{4,3,2,1,0:T(8,128)(2,1)}), bf16[4,2,2,16,2048]{4,3,2,1,0:T(8,128)(2,1)S(1)}, u32[]{:S(2)}, u32[]{:S(2)}) async-start(bf16[4,2,2,16,2048]{4,3,2,1,0:T(8,128)(2,1)} %shard_map.138), calls=%async_computation.2 | async-start | bytes 2097152 | tf_op jit(solution)/shard_map/all_to_all | solution.py:439
  200.1 20.0 %all-to-all-start.3 = ((bf16[4,2,2,16,2048]{4,3,2,1,0:T(8,128)(2,1)}), bf16[4,2,2,16,2048]{4,3,2,1,0:T(8,128)(2,1)S(1)}, u32[]{:S(2)}, u32[]{:S(2)}) async-start(bf16[4,2,2,16,2048]{4,3,2,1,0:T(8,128)(2,1)} %shard_map.139), calls=%async_computation.3 | async-start | bytes 2097152 | tf_op jit(solution)/shard_map/all_to_all | solution.py:439
  204.9 22.7 %collective-permute-start.3 = (bf16[2,16,2048]{2,1,0:T(8,128)(2,1)S(1)}, bf16[2,16,2048]{2,1,0:T(8,128)(2,1)S(1)}, u32[]{:S(2)}, u32[]{:S(2)}) collective-permute-start(bf16[2,16,2048]{2,1,0:T(8,128)(2,1)S(1)} %get-tuple-element.35), channel_id=1, source_target_pairs={{0,248},{8,240},{16,232},{24,224},{32,216},{40,208},{48,200},{56,1... | collective-permute-start | bytes 393224 | tf_op jit(solution)/shard_map/ppermute | solution.py:502
  206.1 21.6 %collective-permute-start.4 = (bf16[2,16,2048]{2,1,0:T(8,128)(2,1)S(1)}, bf16[2,16,2048]{2,1,0:T(8,128)(2,1)S(1)}, u32[]{:S(2)}, u32[]{:S(2)}) collective-permute-start(bf16[2,16,2048]{2,1,0:T(8,128)(2,1)S(1)} %get-tuple-element.35), channel_id=1, source_target_pairs={{0,252},{1,253},{2,254},{3,255},{4,248},{5,249},{6,250},{7,251},{8... | collective-permute-start | bytes 393224 | tf_op jit(solution)/shard_map/ppermute | solution.py:503
  209.6 15.5 %collective-permute-start.2 = (bf16[2,16,2048]{2,1,0:T(8,128)(2,1)S(1)}, bf16[2,16,2048]{2,1,0:T(8,128)(2,1)S(1)}, u32[]{:S(2)}, u32[]{:S(2)}) collective-permute-start(bf16[2,16,2048]{2,1,0:T(8,128)(2,1)S(1)} %get-tuple-element.36), channel_id=1, source_target_pairs={{0,4},{1,5},{2,6},{3,7},{4,0},{5,1},{6,2},{7,3},{8,12},{9,13},{10,... | collective-permute-start | bytes 393224 | tf_op jit(solution)/shard_map/ppermute | solution.py:501
  220.4 18.3 %collective-permute-start.6 = (bf16[2,16,2048]{2,1,0:T(8,128)(2,1)S(1)}, bf16[2,16,2048]{2,1,0:T(8,128)(2,1)S(1)}, u32[]{:S(2)}, u32[]{:S(2)}) collective-permute-start(bf16[2,16,2048]{2,1,0:T(8,128)(2,1)S(1)} %get-tuple-element.31), channel_id=1, source_target_pairs={{0,248},{8,240},{16,232},{24,224},{32,216},{40,208},{48,200},{56,1... | collective-permute-start | bytes 393224 | tf_op jit(solution)/shard_map/ppermute | solution.py:502
  220.5 18.2 %collective-permute-start.7 = (bf16[2,16,2048]{2,1,0:T(8,128)(2,1)S(1)}, bf16[2,16,2048]{2,1,0:T(8,128)(2,1)S(1)}, u32[]{:S(2)}, u32[]{:S(2)}) collective-permute-start(bf16[2,16,2048]{2,1,0:T(8,128)(2,1)S(1)} %get-tuple-element.31), channel_id=1, source_target_pairs={{0,252},{1,253},{2,254},{3,255},{4,248},{5,249},{6,250},{7,251},{8... | collective-permute-start | bytes 393224 | tf_op jit(solution)/shard_map/ppermute | solution.py:503
  225.1 13.6 %collective-permute-start.5 = (bf16[2,16,2048]{2,1,0:T(8,128)(2,1)S(1)}, bf16[2,16,2048]{2,1,0:T(8,128)(2,1)S(1)}, u32[]{:S(2)}, u32[]{:S(2)}) collective-permute-start(bf16[2,16,2048]{2,1,0:T(8,128)(2,1)S(1)} %get-tuple-element.32), channel_id=1, source_target_pairs={{0,4},{1,5},{2,6},{3,7},{4,0},{5,1},{6,2},{7,3},{8,12},{9,13},{10,... | collective-permute-start | bytes 393224 | tf_op jit(solution)/shard_map/ppermute | solution.py:501
  240.4 18.6 %all-to-all-start.4 = ((bf16[4,64,2048]{2,1,0:T(8,128)(2,1)}), bf16[4,64,2048]{2,1,0:T(8,128)(2,1)S(1)}, u32[]{:S(2)}, u32[]{:S(2)}) async-start(bf16[4,64,2048]{2,1,0:T(8,128)(2,1)} %bitcast.23), calls=%async_computation.4 | async-start | bytes 2097152 | tf_op jit(solution)/shard_map/all_to_all | solution.py:439
  259.0 1.0 copy-start.2
  267.7 12.1 %all-to-all-start.5 = ((bf16[4,32,2048]{2,1,0:T(8,128)(2,1)}), bf16[4,32,2048]{2,1,0:T(8,128)(2,1)S(1)}, u32[]{:S(2)}, u32[]{:S(2)}) async-start(bf16[4,32,2048]{2,1,0:T(8,128)(2,1)} %get-tuple-element.17), calls=%async_computation.5 | async-start | bytes 1048576 | tf_op jit(solution)/shard_map/all_to_all | solution.py:439
  280.2 11.5 %all-to-all-start.6 = ((bf16[4,32,2048]{2,1,0:T(8,128)(2,1)}), bf16[4,32,2048]{2,1,0:T(8,128)(2,1)S(1)}, u32[]{:S(2)}, u32[]{:S(2)}) async-start(bf16[4,32,2048]{2,1,0:T(8,128)(2,1)} %get-tuple-element.19), calls=%async_computation.6 | async-start | bytes 1048576 | tf_op jit(solution)/shard_map/all_to_all | solution.py:439
  283.7 14.7 %collective-permute-start.9 = (bf16[64,2048]{1,0:T(8,128)(2,1)S(1)}, bf16[64,2048]{1,0:T(8,128)(2,1)S(1)}, u32[]{:S(2)}, u32[]{:S(2)}) collective-permute-start(bf16[64,2048]{1,0:T(8,128)(2,1)S(1)} %shard_map.142), channel_id=1, source_target_pairs={{0,4},{1,5},{2,6},{3,7},{4,0},{5,1},{6,2},{7,3},{8,12},{9,13},{10,... | collective-permute-start | bytes 786440 | tf_op jit(solution)/shard_map/ppermute | solution.py:553
Sparse Core Ops, SparseCore 0:
  9.2 77.3 all-gather.2
  90.3 68.3 all-gather.4
